TPU v7x, 128 devices: a whole 4x4x4 slice. The times are simulated.
128 devices in a mesh: leaf: 16 (over z, y), help: 8 (over x, core).
Axes of the slice: x: 4, y: 4, z: 4, core: 2. Of those that a mesh axis runs over, the one named last changes fastest.
Arguments:
- points: float32 [64, 131072], P(None, ('leaf', 'help')), may hold values from -3 to 3
- weights: float32 [256, 131072], P(None, ('leaf', 'help')), may hold values from -0.12 to 0.12
- interp: float32 [256, 512, 256], P(('leaf', 'help')), may hold values from -0.25 to 0.25
- transfer: float32 [14, 512, 256], replicated, may hold values from -0.25 to 0.25
- near_count: int32 [16, 16], P('leaf', 'help'), may hold values from 1 to 32, 256 in all within a row
- near_src: int32 [256, 32], P(('leaf', 'help')), may hold values from 0 to 255, as said below
- skel_group: int32 [16, 256], P('leaf'), may hold values from 0 to 8191, as said below
- skel_node: int32 [14, 256], replicated, may hold values from 0 to 511, as said below
- far_nodes: int32 [30, 4], replicated, may hold values from 0 to 15, as said below
Outputs:
- product: float32 [256, 131072], P(None, ('leaf', 'help'))
Inputs may be any that keep to these rules, and one draw needn't show every extreme that they name: `near_src`: slot 0 of leaf i names leaf i itself; every source of a leaf of subtree g is a leaf of subtree g - 1, g or g + 1. Slots at or after the leaf's near_count are not used. `near_count`: the 16 counts of one subtree sum to exactly 256. `skel_group`: each row holds 256 distinct indices into its subtree's points, counted from the subtree's first point. `skel_node`: each row holds 256 distinct indices into its two children's skeleton points, the first child's first. `far_nodes`: rows 0 to 15 are the level-0 nodes, the next 8 rows the level-1 nodes, and so on down to the 2 nodes of the highest listed level; each entry is a node number of that row's level. On level 0, the first entry of node k's row is k - 1 (modulo 16) and no other entry is k, k + 1 or k - 1 (modulo 16); on a higher level of c >= 4 nodes, no entry of node k's row is k, k + 1 or k - 1 (modulo c); on the level of 2 nodes, every entry is the other node.
All inputs are finite; a program needn't handle non-finite values. No bound on the sum of `near_count` on one device may be relied on, other than what follows from the above.
Results may differ from a plain program's by a relative error of at most 0.0003.
Values sent between devices are 32-bit elements; how exact they have to be, the bound alone decides.
A program may use at most 192 MiB of HBM per device.

v0:
```python
from functools import partial

import jax
import jax.numpy as jnp
from jax import lax
from jax.sharding import PartitionSpec as P

F = 64
R = 256
LEAF = 512
SK = 256
NEAR = 32


HIGH = lax.Precision.HIGHEST


def padded(cells, sides, width):
    for axis, dim in sides:
        count = lax.axis_size(axis)
        ends = count - 1
        head = lax.slice_in_dim(cells, 0, width, axis=dim)
        tail = lax.slice_in_dim(cells, cells.shape[dim] - width, cells.shape[dim], axis=dim)
        cells = jnp.concatenate(
            [
                lax.ppermute(tail, axis, [(i, (i + 1) % count) for i in range(ends)]),
                cells,
                lax.ppermute(head, axis, [((i + 1) % count, i) for i in range(ends)]),
            ],
            axis=dim,
        )
    return cells


def from_behind(array, axis, by):
    length = lax.axis_size(axis)
    pairs = [(i, i + by) for i in range(length) if 0 <= i + by < length]
    return lax.ppermute(array, axis, pairs)


def kernel_block(source, target):
    cross = lax.dot_general(
        source, target, (((0,), (0,)), ((), ())), precision=HIGH, preferred_element_type=jnp.float32
    )
    source_sq = jnp.sum(source * source, axis=0)
    target_sq = jnp.sum(target * target, axis=0)
    dist = source_sq[:, None] + target_sq[None, :] - 2.0 * cross
    return jnp.exp((0.5 * F - dist) * 0.25)


def apply_block(source_pts, source_vals, target_pts):
    return jnp.dot(
        source_vals,
        kernel_block(source_pts, target_pts),
        precision=HIGH,
        preferred_element_type=jnp.float32,
    )


def skeleton_term(source, target):
    return apply_block(source[:F], source[F:], target[:F])


def upper_start(level, groups):
    return sum((groups >> step for step in range(1, level)))


def list_start(level, groups):
    return sum((groups >> step for step in range(level)))


def combine(left, right, picks, matrix):
    both_pts = jnp.concatenate([left[:F], right[:F]], axis=1)
    both_vals = jnp.concatenate([left[F:], right[F:]], axis=1)
    chosen = jnp.take(both_pts, picks, axis=1)
    merged = jnp.dot(both_vals, matrix, precision=HIGH, preferred_element_type=jnp.float32)
    return jnp.concatenate([chosen, merged], axis=0)


def add_scaled(value, factor, source, target):
    return value + factor * skeleton_term(source, target)


def keep_scaled(value, factor, source, target):
    return value


def fold_sources(level, helper, helpers, ids, target, total, piece, start):

    def one(index, acc):
        node = index >> level
        aligned = index % (1 << level) == 0
        assigned = node % helpers == helper
        hits = jnp.sum((ids == node).astype(jnp.float32)) * (aligned & assigned).astype(jnp.float32)
        source = lax.dynamic_index_in_dim(piece, index, 0, keepdims=False)
        return lax.cond(hits > 0.0, add_scaled, keep_scaled, acc, hits, source, target)

    return lax.fori_loop(0, piece.shape[0], one, total)


def shards(
    points, weights, interp, transfer, near_count, near_src, skel_group, skel_node, far_nodes
):
    helpers = lax.axis_size("help")
    groups = lax.axis_size("leaf")
    levels = groups.bit_length() - 1
    helper = lax.axis_index("help")
    group = lax.axis_index("leaf")
    own_leaves = interp.shape[0]
    own_cols = points.shape[1]
    cloud = jnp.concatenate([points, weights], axis=0)
    group_cloud = lax.all_gather(cloud, "help", axis=1, tiled=True)
    group_leaves = group_cloud.shape[1] // LEAF
    beside_all = padded(group_cloud, (("leaf", 1),), group_cloud.shape[1])
    leaf_vals = weights.reshape(R, own_leaves, LEAF)
    own_up = jnp.einsum("rjl,jls->rs", leaf_vals, interp, precision=HIGH)
    group_up = lax.psum(own_up, "help")
    group_pts = group_cloud[:F]
    group_skel = jnp.take(group_pts, skel_group[0], axis=1)
    payload = jnp.concatenate([group_skel, group_up], axis=0)
    empty = jnp.zeros((R, SK), jnp.float32)
    far_parts = []
    tiers = [payload]
    for level in range(1, levels):
        right = from_behind(tiers[-1], "leaf", -(1 << level - 1))
        row = upper_start(level, groups) + (group >> level)
        tiers.append(combine(tiers[-1], right, skel_node[row], transfer[row]))
    for level in range(levels):
        ids = far_nodes[list_start(level, groups) + (group >> level)]
        folder = partial(fold_sources, level, helper, helpers, ids, tiers[level])
        far_parts.append(
            folder(
                empty, lax.all_gather(tiers[level][None], "leaf", axis=0, tiled=True), jnp.int32(0)
            )
        )
    far_sums = lax.psum(tuple(far_parts), "help")
    local = far_sums[levels - 1]
    for level in range(levels - 1, 0, -1):
        row = upper_start(level, groups) + (group >> level)
        pushed = lax.dot_general(
            local,
            transfer[row],
            (((1,), (1,)), ((), ())),
            precision=HIGH,
            preferred_element_type=jnp.float32,
        )
        sent = from_behind(pushed[:, SK:], "leaf", 1 << level - 1)
        parent_side = group % (1 << level) == 0
        local = far_sums[level - 1] + jnp.where(parent_side, pushed[:, :SK], sent)
    far_out = jnp.einsum("rs,jls->rjl", local, interp, precision=HIGH).reshape(R, own_cols)
    base = (group - 1) * group_leaves
    counts = near_count[0]

    def own_tile(slot, total):
        leaf = slot // NEAR
        index = slot % NEAR
        column = (near_src[leaf, index] - base) * LEAF
        source = lax.dynamic_slice_in_dim(beside_all, column, LEAF, 1)
        target = lax.dynamic_slice_in_dim(points, leaf * LEAF, LEAF, 1)

        def add_tile(value):
            current = lax.dynamic_slice_in_dim(value, leaf * LEAF, LEAF, 1)
            return lax.dynamic_update_slice_in_dim(
                value, current + apply_block(source[:F], source[F:], target), leaf * LEAF, 1
            )

        return lax.cond(index < counts[leaf], add_tile, lambda value: value, total)

    near_out = lax.fori_loop(0, own_leaves * NEAR, own_tile, jnp.zeros((R, own_cols), jnp.float32))
    return far_out + near_out


def solution(mesh):
    placed = (
        P(None, ("leaf", "help")),
        P(None, ("leaf", "help")),
        P(("leaf", "help"), None, None),
        P(),
        P("leaf", "help"),
        P(("leaf", "help"), None),
        P("leaf", None),
        P(),
        P(),
    )
    return jax.shard_map(
        shards, mesh=mesh, in_specs=placed, out_specs=P(None, ("leaf", "help")), check_vma=False
    )
```

profile of v0, /device:TPU:29, one launch (start us, length us, event | category | flops | bytes accessed | tf_op | source)
XLA Modules:
  0.0 1313.0 jit_solution(16999950385504357284)
XLA Ops:
  14.8 67.2 %all-gather.10.cloned.1.call-done = f32[320,8192]{0,1:T(8,128)} async-done(((f32[320,1024]{0,1:T(8,128)}), f32[320,8192]{0,1:T(8,128)}) %all-gather.10.cloned.1.call-update) | async-done | bytes 10485776 | tf_op jit(solution)/shard_map/all_gather | solution.py:112
  89.4 52.3 %all-reduce.4.cloned.1.call-done = f32[256,256]{1,0:T(8,128)} async-done(((f32[256,256]{1,0:T(8,128)}), f32[256,256]{1,0:T(8,128)}) %all-reduce.4.cloned.1.call-update) | async-done | bytes 262160 | tf_op jit(solution)/shard_map/psum | solution.py:117
  146.7 11.0 collective-permute-done
  163.2 12.5 collective-permute-done.1
  180.5 14.1 %collective-permute-done.2 = f32[320,256]{1,0:T(8,128)S(1)} collective-permute-done((f32[320,256]{1,0:T(8,128)}, f32[320,256]{1,0:T(8,128)S(1)}, u32[]{:S(2)}, u32[]{:S(2)}) %collective-permute-start.2) | collective-permute-done | bytes 327712 | tf_op jit(solution)/shard_map/ppermute | solution.py:38
  198.1 12.0 copy.46
  215.7 24.5 %while.92 = (s32[]{:T(128)}, f32[256,256]{1,0:T(8,128)S(1)}, s32[]{:T(128)}, s32[4]{0:T(128)S(1)}, f32[16,320,256]{2,1,0:T(8,128)}, /*index=5*/f32[64,256]{1,0:T...) while((s32[]{:T(128)}, f32[256,256]{1,0:T(8,128)S(1)}, s32[]{:T(128)}, ...), condition=%wide.region_7.8_spmd, body=%wide.region_1.7_spmd.sunk | while | flops 252182048 | bytes 1578854 | solution.py:98
  240.3 251.0 %all-gather.14.cloned.1.call-done = f32[5120,256]{1,0:T(8,128)} async-done(((f32[320,256]{1,0:T(8,128)}), f32[5120,256]{1,0:T(8,128)}) %all-gather.14.cloned.1.call-update) | async-done | bytes 5242896 | tf_op jit(solution)/shard_map/all_gather | solution.py:133
  491.2 24.5 %while.93 = (s32[]{:T(128)}, f32[256,256]{1,0:T(8,128)S(1)}, s32[]{:T(128)}, s32[4]{0:T(128)S(1)}, f32[16,320,256]{2,1,0:T(8,128)}, /*index=5*/f32[64,256]{1,0:T...) while((s32[]{:T(128)}, f32[256,256]{1,0:T(8,128)S(1)}, ...), condition=%wide.region_15.17_spmd, body=%wide.region_9.16_spmd.sunk | while | flops 252182048 | bytes 1577950 | solution.py:98
  515.8 33.7 %all-gather.16.cloned.1.call-done = f32[5120,256]{1,0:T(8,128)} async-done(((f32[320,256]{1,0:T(8,128)}), f32[5120,256]{1,0:T(8,128)}) %all-gather.16.cloned.1.call-update) | async-done | bytes 5242896 | tf_op jit(solution)/shard_map/all_gather | solution.py:133
  549.5 21.6 %while.94 = (s32[]{:T(128)}, f32[256,256]{1,0:T(8,128)S(1)}, s32[]{:T(128)}, s32[4]{0:T(128)S(1)}, f32[16,320,256]{2,1,0:T(8,128)}, /*index=5*/f32[64,256]{1,0:T...) while((s32[]{:T(128)}, f32[256,256]{1,0:T(8,128)S(1)}, ...), condition=%wide.region_23.25_spmd, body=%wide.region_17.24_spmd.sunk | while | flops 252182048 | bytes 1577966 | solution.py:98
  571.2 36.6 %all-gather.18.cloned.1.call-done = f32[5120,256]{1,0:T(8,128)} async-done(((f32[320,256]{1,0:T(8,128)}), f32[5120,256]{1,0:T(8,128)}) %all-gather.18.cloned.1.call-update) | async-done | bytes 5242896 | tf_op jit(solution)/shard_map/all_gather | solution.py:133
  607.9 21.5 %while.95 = (s32[]{:T(128)}, f32[256,256]{1,0:T(8,128)S(1)}, s32[]{:T(128)}, s32[4]{0:T(128)S(1)}, f32[16,320,256]{2,1,0:T(8,128)}, /*index=5*/f32[64,256]{1,0:T...) while((s32[]{:T(128)}, f32[256,256]{1,0:T(8,128)S(1)}, ...), condition=%wide.region_31.33_spmd, body=%wide.region_25.0_spmd.sunk | while | flops 252182048 | bytes 1577950 | solution.py:98
  630.1 60.3 %all-reduce.6.cloned.1.call-done = (f32[256,256]{1,0:T(8,128)}, f32[256,256]{1,0:T(8,128)}, f32[256,256]{1,0:T(8,128)}, f32[256,256]{1,0:T(8,128)}) async-done(((f32[256,256]{1,0:T(8,128)}, f32[256,256]{1,0:T(8,128)}, f32[256,256]{1,0:T(8,128)}, f32[256,256]{1,0:T(8,128)}), (f32[256,256]{1,0:T(8,128)}, f32[256,256]{1,0:T(8,128)}, f32[256,256]{1,0:T(8,128)}, ...) | async-done | bytes 1048592 | tf_op jit(solution)/shard_map/psum | solution.py:136
  707.9 11.9 copy.48
  719.8 11.9 copy.49
  738.7 34.2 %pad_maximum_fusion = f32[320,24576]{0,1:T(8,128)} fusion(f32[320,8192]{0,1:T(8,128)} %copy.49, f32[320,8192]{0,1:T(8,128)} %all-gather.10.cloned.1.call-done, f32[320,8192]{0,1:T(8,128)} %copy.48), kind=kLoop, calls=%fused_computation.77 | loop fusion | flops 15728640 | bytes 62914560 | tf_op jit(solution)/shard_map/concatenate | solution.py:24
  772.9 34.5 %copy.50 = f32[320,24576]{1,0:T(8,128)} copy(f32[320,24576]{0,1:T(8,128)} %pad_maximum_fusion) | data formatting | bytes 62914560 | tf_op jit(solution)/shard_map/while | solution.py:169
  807.6 494.6 %while.96 = (s32[]{:T(128)}, f32[256,1024]{1,0:T(8,128)S(1)}, s32[2]{0:T(128)S(1)}, s32[2,32]{1,0:T(2,128)S(1)}, s32[]{:T(128)}, /*index=5*/f32[320,24576]{1,0:T...) while((s32[]{:T(128)}, f32[256,1024]{1,0:T(8,128)S(1)}, ...), condition=%wide.region_38.40_spmd, body=%wide.region_33.39_spmd.sunk | while | flops 1008204800 | bytes 4203066 | solution.py:169
  808.7 6.6 conditional.14
  862.8 6.6 conditional.14
  893.7 6.6 conditional.14
  924.6 6.6 conditional.14
  955.5 6.6 conditional.14
  986.5 6.6 conditional.14
  1017.4 6.6 conditional.14
  1048.3 6.6 conditional.14
  1079.2 6.6 conditional.14
  1110.1 6.6 conditional.14
  1141.0 6.6 conditional.14
  1171.9 6.6 conditional.14
  1295.6 6.6 conditional.14
  (624 shorter events, 869.0 us)
Async XLA Ops:
  6.5 6.4 copy-start
  6.5 6.4 copy-start.5
  6.5 8.2 copy-start.11
  6.5 75.4 %all-gather.10.cloned.1.call-start = ((), (), s32[]{:S(2)}) async-start(), calls=%async_computation | async-start | bytes 14155776 | tf_op jit(solution)/shard_map/all_gather | solution.py:112
  12.9 128.7 %all-reduce.4.cloned.1.call-start = ((), (), s32[]{:S(2)}) async-start(), calls=%async_computation.1 | async-start | bytes 524288 | tf_op jit(solution)/shard_map/psum | solution.py:117
  14.7 200.9 %all-gather.12.cloned.1.call-start = ((), (), s32[]{:S(2)}) async-start(), calls=%async_computation.2 | async-start | bytes 5570560 | tf_op jit(solution)/shard_map/all_gather | solution.py:133
  143.4 347.9 %all-gather.14.cloned.1.call-start = ((), (), s32[]{:S(2)}) async-start(), calls=%async_computation.3 | async-start | bytes 5570560 | tf_op jit(solution)/shard_map/all_gather | solution.py:133
  144.2 13.5 %collective-permute-start = (f32[320,256]{1,0:T(8,128)}, f32[320,256]{1,0:T(8,128)S(1)}, u32[]{:S(2)}, u32[]{:S(2)}) collective-permute-start(f32[320,256]{1,0:T(8,128)} %pad_maximum_fusion.2), channel_id=1, source_target_pairs={{8,0},{16,8},{24,16},{32,24},{40,32},{48,40},{56,48},{64,56},{72,6... | collective-permute-start | bytes 983048 | tf_op jit(solution)/shard_map/ppermute | solution.py:38
  161.2 388.3 %all-gather.16.cloned.1.call-start = ((), (), s32[]{:S(2)}) async-start(), calls=%async_computation.4 | async-start | bytes 5570560 | tf_op jit(solution)/shard_map/all_gather | solution.py:133
  161.3 14.4 %collective-permute-start.1 = (f32[320,256]{1,0:T(8,128)}, f32[320,256]{1,0:T(8,128)S(1)}, u32[]{:S(2)}, u32[]{:S(2)}) collective-permute-start(f32[320,256]{1,0:T(8,128)} %pad_maximum_fusion.3), channel_id=1, source_target_pairs={{16,0},{24,8},{32,16},{40,24},{48,32},{56,40},{64,48},{72,56},{80,... | collective-permute-start | bytes 983048 | tf_op jit(solution)/shard_map/ppermute | solution.py:38
  179.2 428.7 %all-gather.18.cloned.1.call-start = ((), (), s32[]{:S(2)}) async-start(), calls=%async_computation.5 | async-start | bytes 5570560 | tf_op jit(solution)/shard_map/all_gather | solution.py:133
  179.2 15.4 %collective-permute-start.2 = (f32[320,256]{1,0:T(8,128)}, f32[320,256]{1,0:T(8,128)S(1)}, u32[]{:S(2)}, u32[]{:S(2)}) collective-permute-start(f32[320,256]{1,0:T(8,128)} %pad_maximum_fusion.4), channel_id=1, source_target_pairs={{32,0},{40,8},{48,16},{56,24},{64,32},{72,40},{80,48},{88,56},{96,... | collective-permute-start | bytes 983048 | tf_op jit(solution)/shard_map/ppermute | solution.py:38
  198.1 17.3 %copy-start.9 = (s32[30,4]{0,1:T(4,128)S(1)}, s32[30,4]{0,1:T(4,128)}, u32[]{:S(2)}) copy-start(s32[30,4]{0,1:T(4,128)} %param.39) | copy-start | bytes 1444
  198.1 492.3 %all-reduce.6.cloned.1.call-start = ((), (), s32[]{:S(2)}) async-start(), calls=%async_computation.6 | async-start | bytes 2097152 | tf_op jit(solution)/shard_map/psum | solution.py:136
  210.1 497.8 %collective-permute-start.6 = (f32[320,8192]{1,0:T(8,128)}, f32[320,8192]{1,0:T(8,128)}, u32[]{:S(2)}, u32[]{:S(2)}) collective-permute-start(f32[320,8192]{1,0:T(8,128)} %copy.46), channel_id=1, source_target_pairs={{0,8},{8,16},{16,24},{24,32},{32,40},{40,48},{48,56},{56,64},{64,7... | collective-permute-start | bytes 31457288 | tf_op jit(solution)/shard_map/ppermute | solution.py:26
  212.0 507.8 %collective-permute-start.7 = (f32[320,8192]{1,0:T(8,128)}, f32[320,8192]{1,0:T(8,128)}, u32[]{:S(2)}, u32[]{:S(2)}) collective-permute-start(f32[320,8192]{1,0:T(8,128)} %copy.46), channel_id=1, source_target_pairs={{8,0},{16,8},{24,16},{32,24},{40,32},{48,40},{56,48},{64,56},{72,6... | collective-permute-start | bytes 31457288 | tf_op jit(solution)/shard_map/ppermute | solution.py:28
  240.2 309.3 %copy-start.1 = (f32[256,256]{1,0:T(8,128)}, f32[256,256]{1,0:T(8,128)S(1)}, u32[]{:S(2)}) copy-start(f32[256,256]{1,0:T(8,128)S(1)} %get-tuple-element.1249) | copy-start | bytes 786436
  515.8 92.1 %copy-start.2 = (f32[256,256]{1,0:T(8,128)}, f32[256,256]{1,0:T(8,128)S(1)}, u32[]{:S(2)}) copy-start(f32[256,256]{1,0:T(8,128)S(1)} %get-tuple-element.1250) | copy-start | bytes 786436
  571.2 58.1 %copy-start.3 = (f32[256,256]{1,0:T(8,128)}, f32[256,256]{1,0:T(8,128)S(1)}, u32[]{:S(2)}) copy-start(f32[256,256]{1,0:T(8,128)S(1)} %get-tuple-element.1251) | copy-start | bytes 786436
  629.3 0.7 copy-start.4
  692.1 8.8 collective-permute-start.3
  702.8 29.0 %collective-permute-start.4 = (f32[256,256]{1,0:T(8,128)S(1)}, f32[256,256]{1,0:T(8,128)S(1)}, u32[]{:S(2)}, u32[]{:S(2)}) collective-permute-start(f32[256,256]{1,0:T(8,128)S(1)} %slice.152), channel_id=1, source_target_pairs={{0,16},{8,24},{16,32},{24,40},{32,48},{40,56},{48,64},{56,72},{64,... | collective-permute-start | bytes 786440 | tf_op jit(solution)/shard_map/ppermute | solution.py:38
  719.8 11.9 copy-start.8
  733.4 0.8 copy-start.7
  735.0 567.6 %collective-permute-start.5 = (f32[256,256]{1,0:T(8,128)}, f32[256,256]{1,0:T(8,128)}, u32[]{:S(2)}, u32[]{:S(2)}) collective-permute-start(f32[256,256]{1,0:T(8,128)} %slice.154), channel_id=1, source_target_pairs={{0,8},{8,16},{16,24},{24,32},{32,40},{40,48},{48,56},{56,64},{64,7... | collective-permute-start | bytes 786440 | tf_op jit(solution)/shard_map/ppermute | solution.py:38
  772.9 34.6 %copy-start.6 = (f32[64,1024]{1,0:T(8,128)S(1)}, f32[64,1024]{1,0:T(8,128)}, u32[]{:S(2)}) copy-start(f32[64,1024]{1,0:T(8,128)} %param.31) | copy-start | bytes 786436
  772.9 34.6 %copy-start.10 = (s32[2,32]{1,0:T(2,128)S(1)}, s32[2,32]{1,0:T(2,128)}, u32[]{:S(2)}) copy-start(s32[2,32]{1,0:T(2,128)} %param.36) | copy-start | bytes 772
  772.9 34.6 %copy-start.12 = (s32[1,2]{1,0:T(1,128)S(1)}, s32[1,2]{1,0:T(1,128)}, u32[]{:S(2)}) copy-start(s32[1,2]{1,0:T(1,128)} %param.35) | copy-start | bytes 28
Sparse Core Ops, SparseCore 0:
  13.0 68.9 all-gather.9
  84.3 57.3 all-reduce.3
  144.0 68.5 all-gather.11
  214.8 276.3 all-gather.13
  493.4 56.0 all-gather.15
  551.7 56.0 all-gather.17
  630.2 60.1 all-reduce.5
where the time goes:
time: 1320 us; the launch traced here: 1310 us
  waiting for transfers between devices  544 us (41%)
  matrix products  289 us (22%)
  local copies, waits for them, and re-layouts  168 us (13%)
  other arithmetic  144 us (11%)
  loops' own time  130 us (10%)
  starting transfers between devices  23.3 us (2%)
  between operations  14.1 us (1%)
    all_gather x4, waiting for transfers between devices, shards(): lax.all_gather(tiers[level][None], 'leaf', axis=0, tiled=True)  321 us
    dot_general x66, matrix products, kernel_block(): lax.dot_general(source, target, (((0,), (0,)), ((), ())), precision=HIGH,...  138 us
    dot_general x66, matrix products, apply_block(): jnp.dot(source_vals, kernel_block(source_pts, target_pts), precision=HIGH...  137 us
    all_gather x1, waiting for transfers between devices, shards(): group_cloud = lax.all_gather(cloud, 'help', axis=1, tiled=True)  67.2 us
    reduce_sum x66, other arithmetic, kernel_block(): target_sq = jnp.sum(target * target, axis=0)  62.2 us
    psum x1, waiting for transfers between devices, shards(): far_sums = lax.psum(tuple(far_parts), 'help')  60.3 us
    psum x1, waiting for transfers between devices, shards(): group_up = lax.psum(own_up, 'help')  52.3 us
    another operation x64, loops' own time, own_tile(): return lax.cond(index < counts[leaf], add_tile, lambda value: value, total)  47.3 us
  transfers between devices with their start and end apart: 15, of which 10 were waited for; matrix products, arithmetic and copies ran while one was open for 45% of the time, Pallas kernels for 0%

commit v1 on v0

v1 whole, which is shorter than its diff:
```python
import jax
import jax.numpy as jnp
from jax import lax
from jax.experimental import pallas as pl
from jax.experimental.pallas import tpu as pltpu
from jax.sharding import PartitionSpec as P

F = 64
R = 256
LEAF = 512
SK = 256
NEAR = 32
GROUPS = 16
HELP = 8
OWN = 2
COLS = OWN * LEAF
XS = 4
LEVELS = 4
UPPER = 14
STARTS = (0, 16, 24, 28)
NODES = 30
ROWS = R // HELP
PROWS = F // HELP
PACK = ROWS + PROWS
PARTS = 1 + R // F
ROOT_HALF = 0.7071067811865476

BF = jnp.bfloat16
F32 = jnp.float32
MESH = pl.DeviceIdType.MESH


def halves(value):
    high = value.astype(BF)
    return high, (value - high.astype(F32)).astype(BF)


def mul(left, right):
    return jnp.dot(left, right, preferred_element_type=F32)


def mul_t(left, right):
    return lax.dot_general(left, right, (((1,), (1,)), ((), ())), preferred_element_type=F32)


def product3(left, right, dot=mul):
    left_hi, left_lo = halves(left)
    right_hi, right_lo = halves(right)
    return dot(left_hi, right_hi) + dot(left_lo, right_hi) + dot(left_hi, right_lo)


def stacked_halves(pts):
    scaled = pts * ROOT_HALF
    high = scaled.astype(BF).astype(F32)
    low = (scaled - high).astype(BF).astype(F32)
    return jnp.concatenate([high, low], axis=0)


def target_side(both):
    high, low = both[:F], both[F:]
    whole = high + low
    own = 4.0 - 0.5 * jnp.sum(whole * whole, axis=0, keepdims=True)
    high, low = high.astype(BF), low.astype(BF)
    return jnp.concatenate([high, high, low, low], axis=0), own


def source_side(both):
    turned = both.T
    whole = turned[:, :F] + turned[:, F:]
    own = 4.0 - 0.5 * jnp.sum(whole * whole, axis=1, keepdims=True)
    turned = turned.astype(BF)
    return jnp.concatenate([turned, turned], axis=1), own


def remote(src, dst, send, recv, group, helper):
    return pltpu.make_async_remote_copy(
        src_ref=src,
        dst_ref=dst,
        send_sem=send,
        recv_sem=recv,
        device_id=(group, helper),
        device_id_type=MESH,
    )


def spread_kernel(
    pts, wts, interp, transfer, skg, skn, far, meta,
    cloud, tgt, metas, far_out,
    tr, rs_send, rs_buf, lf_send, lf_buf, p_send, p_buf, tier_u, tier_z, v_buf,
    load_sem, y_send, y_recv, f_send, f_recv, s_send, s_recv, own_sem,
    t_send, t_recv, m_send, m_recv, rs_ss, rs_rs, lf_ss, lf_rs, p_ss, p_rs, v_ss, v_rs,
):
    g = lax.axis_index("leaf")
    h = lax.axis_index("help")
    x = lax.div(h, 2)
    core = lax.rem(h, 2)
    sib = h + 1 - 2 * core
    after = lax.rem(g + 1, GROUPS)
    before = lax.rem(g + GROUPS - 1, GROUPS)

    def helper_at(d):
        return lax.rem(h + d, HELP)

    def group_at(d):
        return lax.rem(g + d, GROUPS)

    load = pltpu.make_async_copy(transfer, tr, load_sem)
    load.start()

    barrier = pltpu.get_barrier_semaphore()

    @pl.loop(1, HELP)
    def _(d):
        pl.semaphore_signal(barrier, inc=1, device_id=(g, helper_at(d)), device_id_type=MESH)

    @pl.loop(1, GROUPS)
    def _(d):
        pl.semaphore_signal(barrier, inc=1, device_id=(group_at(d), h), device_id_type=MESH)

    pl.semaphore_wait(barrier, HELP + GROUPS - 2)

    def part(i):
        return pts if i == 0 else wts.at[pl.ds(F * (i - 1), F)]

    def y_copy(way, i):
        where = after if way == 0 else before
        return remote(
            part(i), cloud.at[2 * way, core, i], y_send.at[way, i], y_recv.at[way, i], where, h
        )

    def f_copy(way, i):
        spot = cloud.at[2 * way, core, i]
        return remote(spot, spot, f_send.at[way, i], f_recv.at[way, i], g, sib)

    def s_copy(i):
        return remote(part(i), cloud.at[1, core, i], s_send.at[i], s_recv.at[i], g, sib)

    def own_copy(i):
        return pltpu.make_async_copy(part(i), cloud.at[1, core, i], own_sem.at[i])

    def x_at(d):
        return lax.rem(x + d, XS) * 2 + core

    def t_copy(d):
        return remote(pts, tgt.at[x], t_send.at[d], t_recv.at[d], g, x_at(d))

    def m_copy(d):
        return remote(meta, metas.at[x], m_send.at[d], m_recv.at[d], g, x_at(d))

    own_t = pltpu.make_async_copy(pts, tgt.at[x], own_sem.at[PARTS])
    own_m = pltpu.make_async_copy(meta, metas.at[x], own_sem.at[PARTS + 1])

    for i in range(PARTS):
        y_copy(0, i).start()
        y_copy(1, i).start()

    picks = skg[...] - h * COLS
    onehot = (lax.broadcasted_iota(jnp.int32, (COLS, SK), 0) == picks).astype(BF)
    own_pts = pts[...]
    first, rest = halves(own_pts)
    second = (own_pts - first.astype(F32)).astype(BF)
    third = (own_pts - first.astype(F32) - second.astype(F32)).astype(BF)
    del rest
    chosen = mul(first, onehot) + mul(second, onehot) + mul(third, onehot)
    up = product3(wts[...], interp[...].reshape(COLS, SK))
    rs_send[:, :ROWS, :] = up.reshape(HELP, ROWS, SK)
    rs_send[:, ROWS:, :] = chosen.reshape(HELP, PROWS, SK)

    def rs_copy(d):
        to = helper_at(d)
        return remote(rs_send.at[to], rs_buf.at[h], rs_ss.at[d], rs_rs.at[d], g, to)

    @pl.loop(1, HELP)
    def _(d):
        rs_copy(d).start()

    for d in range(1, XS):
        t_copy(d).start()
        m_copy(d).start()
    for i in range(PARTS):
        s_copy(i).start()
        own_copy(i).start()
    own_t.start()
    own_m.start()

    @pl.loop(1, HELP)
    def _(d):
        rs_copy(d).wait_recv()

    rs_buf[h] = rs_send[h]
    total = rs_buf[0]
    for i in range(1, HELP):
        total = total + rs_buf[i]
    lf_send[...] = total

    def lf_copy(d):
        return remote(lf_send, lf_buf.at[g], lf_ss.at[d], lf_rs.at[d], group_at(d), h)

    @pl.loop(1, GROUPS)
    def _(d):
        lf_copy(d).start()

    lf_buf[g] = total
    load.wait()

    @pl.loop(1, GROUPS)
    def _(d):
        lf_copy(d).wait_recv()

    p_send[...] = lf_buf[:, ROWS:, :]

    def p_copy(d):
        return remote(p_send, p_buf.at[h], p_ss.at[d], p_rs.at[d], g, helper_at(d))

    @pl.loop(1, HELP)
    def _(d):
        p_copy(d).start()

    p_buf[h] = p_send[...]

    tier_u[:GROUPS] = lf_buf[:, :ROWS, :]

    @pl.loop(0, UPPER)
    def _(r):
        both = jnp.concatenate([tier_u[2 * r], tier_u[2 * r + 1]], axis=1)
        tier_u[GROUPS + r] = product3(both, tr[r])

    @pl.loop(1, HELP)
    def _(d):
        p_copy(d).wait_recv()

    @pl.loop(0, GROUPS)
    def _(n):
        tier_z[n] = stacked_halves(p_buf[:, n].reshape(F, SK)).astype(BF)

    rows = lax.broadcasted_iota(jnp.int32, (2 * SK, SK), 0)

    @pl.loop(0, UPPER)
    def _(r):
        both = jnp.concatenate([tier_z[2 * r], tier_z[2 * r + 1]], axis=1)
        pick = (rows == skn[pl.ds(r, 1), :]).astype(BF)
        tier_z[GROUPS + r] = mul(both, pick).astype(BF)

    sums = []
    for level in range(LEVELS):
        q = STARTS[level] + lax.shift_right_logical(g, level)
        right, target_own = target_side(tier_z[q].astype(F32))

        def one(slot, acc, level=level, q=q, right=right, target_own=target_own):
            node = STARTS[level] + far[q, slot]
            left, source_own = source_side(tier_z[node].astype(F32))
            block = jnp.exp(mul(left, right) + source_own + target_own)
            return acc + product3(tier_u[node], block)

        sums.append(lax.fori_loop(0, 4, one, jnp.zeros((ROWS, SK), F32)))

    local = sums[LEVELS - 1]
    for level in range(LEVELS - 1, 0, -1):
        r = STARTS[level] - GROUPS + lax.shift_right_logical(g, level)
        side = lax.rem(lax.shift_right_logical(g, level - 1), 2)
        half = tr[r, pl.ds(pl.multiple_of(side * SK, SK), SK), :]
        local = sums[level - 1] + product3(local, half, mul_t)
    v_buf[h] = local

    def v_copy(d):
        return remote(v_buf.at[h], v_buf.at[h], v_ss.at[d], v_rs.at[d], g, helper_at(d))

    @pl.loop(1, HELP)
    def _(d):
        v_copy(d).start()

    for i in range(PARTS):
        for way in range(2):
            y_copy(way, i).wait_recv()
            f_copy(way, i).start()

    @pl.loop(1, HELP)
    def _(d):
        v_copy(d).wait_recv()

    far_out[...] = product3(v_buf[...].reshape(R, SK), interp[...].reshape(COLS, SK), mul_t)

    for i in range(PARTS):
        for way in range(2):
            f_copy(way, i).wait()
            y_copy(way, i).wait_send()
        s_copy(i).wait()
        own_copy(i).wait()
    for d in range(1, XS):
        t_copy(d).wait()
        m_copy(d).wait()
    own_t.wait()
    own_m.wait()

    @pl.loop(1, HELP)
    def _(d):
        rs_copy(d).wait_send()
        p_copy(d).wait_send()
        v_copy(d).wait_send()

    @pl.loop(1, GROUPS)
    def _(d):
        lf_copy(d).wait_send()


def spread(points, weights, interp, transfer, skel_group, skel_node, far_nodes, meta):
    vmem = pl.BlockSpec(memory_space=pltpu.VMEM)
    smem = pl.BlockSpec(memory_space=pltpu.SMEM)
    anym = pl.BlockSpec(memory_space=pl.ANY)
    dma = pltpu.SemaphoreType.DMA
    return pl.pallas_call(
        spread_kernel,
        out_shape=(
            jax.ShapeDtypeStruct((3, 2, PARTS, F, COLS), F32),
            jax.ShapeDtypeStruct((XS, F, COLS), F32),
            jax.ShapeDtypeStruct((XS, 8, 128), jnp.int32),
            jax.ShapeDtypeStruct((R, COLS), F32),
        ),
        in_specs=[vmem, vmem, vmem, anym, vmem, vmem, smem, vmem],
        out_specs=(anym, anym, anym, vmem),
        scratch_shapes=[
            pltpu.VMEM((UPPER, 2 * SK, SK), F32),
            pltpu.VMEM((HELP, PACK, SK), F32),
            pltpu.VMEM((HELP, PACK, SK), F32),
            pltpu.VMEM((PACK, SK), F32),
            pltpu.VMEM((GROUPS, PACK, SK), F32),
            pltpu.VMEM((GROUPS, PROWS, SK), F32),
            pltpu.VMEM((HELP, GROUPS, PROWS, SK), F32),
            pltpu.VMEM((NODES, ROWS, SK), F32),
            pltpu.VMEM((NODES, 2 * F, SK), BF),
            pltpu.VMEM((HELP, ROWS, SK), F32),
            dma,
            dma((2, PARTS)), dma((2, PARTS)),
            dma((2, PARTS)), dma((2, PARTS)),
            dma((PARTS,)), dma((PARTS,)),
            dma((PARTS + 2,)),
            dma((XS,)), dma((XS,)),
            dma((XS,)), dma((XS,)),
            dma((HELP,)), dma((HELP,)),
            dma((GROUPS,)), dma((GROUPS,)),
            dma((HELP,)), dma((HELP,)),
            dma((HELP,)), dma((HELP,)),
        ],
        compiler_params=pltpu.CompilerParams(
            collective_id=0, has_side_effects=True, vmem_limit_bytes=40 << 20
        ),
        name="spread",
    )(points, weights, interp, transfer, skel_group, skel_node, far_nodes, meta)


SRC = 3 * 2 * OWN
TGT = XS * OWN


def near_kernel(times, logs, cloud, tgt, part, w_hi, w_lo, left, source_own, right, target_own):
    @pl.loop(0, 6)
    def _(pair):
        step, core = lax.div(pair, 2), lax.rem(pair, 2)
        for j in range(OWN):
            span = slice(j * LEAF, (j + 1) * LEAF)
            s = pair * OWN + j
            for i in range(R // F):
                high, low = halves(cloud[step, core, 1 + i, :, span])
                w_hi[s, i * F:(i + 1) * F, :] = high
                w_lo[s, i * F:(i + 1) * F, :] = low
            factor, own = source_side(stacked_halves(cloud[step, core, 0, :, span]))
            left[s] = factor
            source_own[s] = jnp.broadcast_to(own, (LEAF, 128))

    @pl.loop(0, XS)
    def _(at):
        for j in range(OWN):
            factor, own = target_side(stacked_halves(tgt[at, :, j * LEAF:(j + 1) * LEAF]))
            right[at * OWN + j] = factor
            target_own[at * OWN + j] = jnp.broadcast_to(own, (8, LEAF))

    @pl.loop(0, XS)
    def _(at):
        for j in range(OWN):
            t = at * OWN + j
            part[at, :, j * LEAF:(j + 1) * LEAF] = jnp.zeros((R, LEAF), F32)

            @pl.loop(0, SRC)
            def _(s, t=t, j=j):
                @pl.when(times[t * SRC + s] > 0)
                def _():
                    log = logs[t * SRC + s]
                    own = source_own[s]
                    for c in range(2):
                        span = slice(c * 256, (c + 1) * 256)
                        cross = mul(left[s], right[t, :, span])
                        shift = target_own[t, 0:1, span] + log
                        block = jnp.exp(cross + jnp.concatenate([own, own], axis=1) + shift)
                        high, low = halves(block)
                        where = slice(j * LEAF + c * 256, j * LEAF + (c + 1) * 256)
                        part[at, :, where] += (
                            mul(w_hi[s], high) + mul(w_lo[s], high) + mul(w_hi[s], low)
                        )


def near(times, logs, cloud, tgt):
    vmem = pl.BlockSpec(memory_space=pltpu.VMEM)
    smem = pl.BlockSpec(memory_space=pltpu.SMEM)
    return pl.pallas_call(
        near_kernel,
        out_shape=jax.ShapeDtypeStruct((XS, R, COLS), F32),
        in_specs=[smem, smem, vmem, vmem],
        out_specs=vmem,
        scratch_shapes=[
            pltpu.VMEM((SRC, R, LEAF), BF),
            pltpu.VMEM((SRC, R, LEAF), BF),
            pltpu.VMEM((SRC, LEAF, 4 * F), BF),
            pltpu.VMEM((SRC, LEAF, 128), F32),
            pltpu.VMEM((TGT, 4 * F, LEAF), BF),
            pltpu.VMEM((TGT, 8, LEAF), F32),
        ],
        compiler_params=pltpu.CompilerParams(vmem_limit_bytes=48 << 20),
        name="near",
    )(times, logs, cloud, tgt)


HALF = R // 2


def fold_kernel(part, far_out, out, first, last, first_ss, first_rs, last_ss, last_rs):
    g = lax.axis_index("leaf")
    h = lax.axis_index("help")
    x = lax.div(h, 2)
    core = lax.rem(h, 2)

    def x_at(d):
        return lax.rem(x + d, XS)

    def to(way):
        return x_at(1 if way == 0 else 3) * 2 + core

    barrier = pltpu.get_barrier_semaphore()
    for way in range(2):
        pl.semaphore_signal(barrier, inc=1, device_id=(g, to(way)), device_id_type=MESH)
    pl.semaphore_wait(barrier, 2)

    def rows(i):
        return pl.ds(i * HALF, HALF)

    def first_copy(way):
        src = part.at[x_at(2), rows(way)]
        return remote(src, first.at[way], first_ss.at[way], first_rs.at[way], g, to(way))

    def plain_copy(way):
        src = part.at[x_at(1 if way == 0 else 3), rows(1 - way)]
        dst = last.at[way, rows(1 - way)]
        return remote(src, dst, last_ss.at[way, 0], last_rs.at[way, 0], g, to(way))

    def sum_copy(way):
        dst = last.at[way, rows(way)]
        return remote(first.at[way], dst, last_ss.at[way, 1], last_rs.at[way, 1], g, to(way))

    for way in range(2):
        first_copy(way).start()
    for way in range(2):
        plain_copy(way).start()
    out[...] = far_out[...] + part[x]
    for way in range(2):
        first_copy(way).wait_recv()
        first[way] += part[x_at(1 if way == 0 else 3), rows(way), :]
        sum_copy(way).start()
    for way in range(2):
        plain_copy(way).wait_recv()
    out[rows(1), :] += last[0, rows(1), :]
    out[rows(0), :] += last[1, rows(0), :]
    for way in range(2):
        sum_copy(way).wait_recv()
    out[rows(0), :] += last[0, rows(0), :]
    out[rows(1), :] += last[1, rows(1), :]
    for way in range(2):
        first_copy(way).wait_send()
        plain_copy(way).wait_send()
        sum_copy(way).wait_send()


def fold(part, far_out):
    vmem = pl.BlockSpec(memory_space=pltpu.VMEM)
    dma = pltpu.SemaphoreType.DMA
    return pl.pallas_call(
        fold_kernel,
        out_shape=jax.ShapeDtypeStruct((R, COLS), F32),
        in_specs=[vmem, vmem],
        out_specs=vmem,
        scratch_shapes=[
            pltpu.VMEM((2, HALF, COLS), F32),
            pltpu.VMEM((2, R, COLS), F32),
            dma((2,)), dma((2,)), dma((2, 2)), dma((2, 2)),
        ],
        compiler_params=pltpu.CompilerParams(
            collective_id=1, has_side_effects=True, vmem_limit_bytes=24 << 20
        ),
        name="fold",
    )(part, far_out)


def shards(
    points, weights, interp, transfer, near_count, near_src, skel_group, skel_node, far_nodes
):
    g = lax.axis_index("leaf")
    x = lax.axis_index("help") // 2
    listed = jnp.where(lax.iota(jnp.int32, NEAR)[None, :] < near_count[0][:, None], near_src, -1)
    meta = jnp.pad(listed, ((0, 8 - OWN), (0, 128 - NEAR)), constant_values=-1)
    cloud, tgt, metas, far_out = spread(
        points, weights, interp, transfer, skel_group, skel_node, far_nodes, meta
    )
    slots = metas[:, :OWN, :NEAR].reshape(TGT, 1, NEAR)
    step = lax.iota(jnp.int32, SRC)
    ids = (g - 1 + step // 4) * 16 + x * 4 + step % 4
    ids = jnp.where(ids < 0, -2, ids)
    times = jnp.sum((slots == ids[None, :, None]).astype(jnp.int32), axis=2).reshape(-1)
    logs = jnp.log(jnp.maximum(times, 1).astype(F32))
    part = near(times, logs, cloud, tgt)
    return fold(part, far_out)


def solution(mesh):
    placed = (
        P(None, ("leaf", "help")),
        P(None, ("leaf", "help")),
        P(("leaf", "help"), None, None),
        P(),
        P("leaf", "help"),
        P(("leaf", "help"), None),
        P("leaf", None),
        P(),
        P(),
    )
    return jax.shard_map(
        shards, mesh=mesh, in_specs=placed, out_specs=P(None, ("leaf", "help")), check_vma=False
    )
```

time: 1320 us -> 158 us (0.12)
  the two profiles are of different devices: /device:TPU:29 before, /device:TPU:1 now
where the time goes in v1:
time: 158 us; the launch traced here: 157 us
  Pallas kernels  146 us (92%)
  local copies, waits for them, and re-layouts  9.79 us (6%)
    pallas_call x1, Pallas kernels, spread(): pl.pallas_call(spread_kernel, out_shape=(jax.ShapeDtypeStruct((3, 2, PART...  79.9 us
    pallas_call x1, Pallas kernels, fold(): pl.pallas_call(fold_kernel, out_shape=jax.ShapeDtypeStruct((R, COLS), F32...  37 us
    pallas_call x1, Pallas kernels, near(): pl.pallas_call(near_kernel, out_shape=jax.ShapeDtypeStruct((XS, R, COLS),...  28.9 us
    unnamed x14, local copies, waits for them, and re-layouts  9.62 us

profile of v1, /device:TPU:1, one launch (start us, length us, event | category | flops | bytes accessed | tf_op | source)
XLA Modules:
  0.0 156.7 jit_solution(13622829428560095353)
XLA Ops:
  0.0 0.8 compare_select_fusion.1
  0.8 0.8 copy.11.far
  1.5 0.0 copy-start
  1.5 3.1 %copy-done = f32[14,512,256]{2,1,0:T(8,128)S(1)} copy-done((f32[14,512,256]{2,1,0:T(8,128)S(1)}, f32[14,512,256]{2,1,0:T(8,128)}, u32[]{:S(2)}) %copy-start) | copy-done | bytes 7340056
  4.6 0.0 copy-start.1
  4.6 1.2 copy-done.1
  5.9 0.0 copy-start.2
  5.9 1.2 copy-done.2
  7.1 0.0 copy-start.3
  7.1 0.9 copy-done.3
  8.0 0.0 copy-start.4
  8.0 0.7 copy-done.4
  8.7 0.0 copy-start.5
  8.7 0.7 copy-done.5
  9.4 79.9 %spread.1 = (f32[3,2,5,64,1024]{4,3,2,1,0:T(8,128)}, f32[4,64,1024]{2,1,0:T(8,128)S(1)}, s32[4,8,128]{2,1,0:T(8,128)S(1)}, f32[256,1024]{1,0:T(8,128)S(1)}) custom-call(f32[64,1024]{1,0:T(8,128)S(1)} %copy-done.3, f32[256,1024]{1,0:T(8,128)S(1)} %copy-done.1, f32[2,512,256]{2,1,0:T(8,128)S(1)} %copy-done.2, f32[14,512,256]{2,1,0:T(8,128)S(1)} %copy-done, ...), custom_call_target="tpu_custom_call" | custom-call | tf_op jit(solution)/shard_map/spread/pallas_call | solution.py:311
  89.3 0.3 convert_reduce_fusion
  89.7 0.1 copy.12
  89.8 0.1 reshape.32.times
  89.9 28.9 %near.1.part = f32[4,256,1024]{2,1,0:T(8,128)S(1)} custom-call(s32[96]{0:T(128)S(1)} %reshape.32.times, f32[96]{0:T(128)S(1)} %convert_log_fusion.logs, f32[3,2,5,64,1024]{4,3,2,1,0:T(8,128)} %get-tuple-element.10.cloud, f32[4,64,1024]{2,1,0:T(8,128)S(1)} %get-tuple-element.11.tgt), custom_call_target="tpu_custom_call" | custom-call | tf_op jit(solution)/shard_map/near/pallas_call | solution.py:404
  118.7 37.0 %fold.1 = f32[256,1024]{1,0:T(8,128)S(1)} custom-call(f32[4,256,1024]{2,1,0:T(8,128)S(1)} %near.1.part, f32[256,1024]{1,0:T(8,128)S(1)} %get-tuple-element.12.far_out), custom_call_target="tpu_custom_call" | custom-call | tf_op jit(solution)/shard_map/fold/pallas_call | solution.py:484
  155.8 1.0 copy.14
  (4 shorter events, 0.0 us)
Async XLA Ops:
  1.5 3.1 %copy-start = (f32[14,512,256]{2,1,0:T(8,128)S(1)}, f32[14,512,256]{2,1,0:T(8,128)}, u32[]{:S(2)}) copy-start(f32[14,512,256]{2,1,0:T(8,128)} %transfer.1) | copy-start | bytes 22020100
  4.6 1.2 copy-start.1
  5.9 1.2 copy-start.2
  7.1 0.9 copy-start.3
  8.0 0.7 copy-start.4
  8.7 0.7 copy-start.5

commit v2 on v1

v2 whole, which is shorter than its diff:
```python
import jax
import jax.numpy as jnp
from jax import lax
from jax.experimental import pallas as pl
from jax.experimental.pallas import tpu as pltpu
from jax.sharding import PartitionSpec as P

F = 64
R = 256
LEAF = 512
SK = 256
NEAR = 32
GROUPS = 16
HELP = 8
OWN = 2
COLS = OWN * LEAF
XS = 4
LEVELS = 4
UPPER = 14
STARTS = (0, 16, 24, 28)
NODES = 30
ROWS = R // HELP
PROWS = F // HELP
PARTS = 1 + R // F
ROOT = 0.8493218002880191
PEAK = 5.770780163555854

BF = jnp.bfloat16
F32 = jnp.float32
MESH = pl.DeviceIdType.MESH


def halves(value):
    high = value.astype(BF)
    return high, (value - high.astype(F32)).astype(BF)


def mul(left, right):
    return jnp.dot(left, right, preferred_element_type=F32)


def mul_t(left, right):
    return lax.dot_general(left, right, (((1,), (1,)), ((), ())), preferred_element_type=F32)


def product3(left, right, dot=mul):
    left_hi, left_lo = halves(left)
    right_hi, right_lo = halves(right)
    return dot(left_hi, right_hi) + dot(left_lo, right_hi) + dot(left_hi, right_lo)


def stacked_halves(pts):
    scaled = pts * ROOT
    high = scaled.astype(BF).astype(F32)
    low = (scaled - high).astype(BF).astype(F32)
    return jnp.concatenate([high, low], axis=0)


def target_side(both):
    high, low = both[:F], both[F:]
    whole = high + low
    own = PEAK - 0.5 * jnp.sum(whole * whole, axis=0, keepdims=True)
    high, low = high.astype(BF), low.astype(BF)
    return jnp.concatenate([high, high, low, low], axis=0), own


def source_side(both):
    turned = both.T
    whole = turned[:, :F] + turned[:, F:]
    own = PEAK - 0.5 * jnp.sum(whole * whole, axis=1, keepdims=True)
    turned = turned.astype(BF)
    return jnp.concatenate([turned, turned], axis=1), own


def remote(src, dst, send, recv, group, helper):
    return pltpu.make_async_remote_copy(
        src_ref=src,
        dst_ref=dst,
        send_sem=send,
        recv_sem=recv,
        device_id=(group, helper),
        device_id_type=MESH,
    )


def spread_kernel(
    pts, wts, interp, transfer, skg, skn, far, meta,
    cloud, tgt, metas, far_out,
    pts_v, wts_v, int_v, tr, skg_v, skn_v, far_s,
    ps_send, ps_buf, us_send, us_buf, lp_send, lp_buf, lu_send, p_buf, tier_u, tier_z, v_buf,
    load_sem, y_send, y_recv, f_send, f_recv, s_send, s_recv, own_sem,
    t_send, t_recv, m_send, m_recv,
    ps_ss, ps_rs, us_ss, us_rs, lp_ss, lp_rs, lu_ss, lu_rs, p_ss, p_rs, v_ss, v_rs,
):
    g = lax.axis_index("leaf")
    h = lax.axis_index("help")
    x = lax.div(h, 2)
    core = lax.rem(h, 2)
    sib = h + 1 - 2 * core
    after = lax.rem(g + 1, GROUPS)
    before = lax.rem(g + GROUPS - 1, GROUPS)

    def helper_at(d):
        return lax.rem(h + d, HELP)

    def group_at(d):
        return lax.rem(g + d, GROUPS)

    barrier = pltpu.get_barrier_semaphore()

    @pl.loop(1, HELP)
    def _(d):
        pl.semaphore_signal(barrier, inc=1, device_id=(g, helper_at(d)), device_id_type=MESH)

    @pl.loop(1, GROUPS)
    def _(d):
        pl.semaphore_signal(barrier, inc=1, device_id=(group_at(d), h), device_id_type=MESH)

    pairs = (
        (pts, pts_v), (skg, skg_v), (wts, wts_v), (interp, int_v),
        (far, far_s), (skn, skn_v), (transfer, tr),
    )
    loads = [
        pltpu.make_async_copy(src, dst, load_sem.at[i]) for i, (src, dst) in enumerate(pairs)
    ]
    for copy in loads:
        copy.start()

    def part(i):
        return pts if i == 0 else wts.at[pl.ds(F * (i - 1), F)]

    def y_copy(way, i):
        where = after if way == 0 else before
        return remote(
            part(i), cloud.at[2 * way, core, i], y_send.at[way, i], y_recv.at[way, i], where, h
        )

    def f_copy(way, i):
        spot = cloud.at[2 * way, core, i]
        return remote(spot, spot, f_send.at[way, i], f_recv.at[way, i], g, sib)

    sends = (g < GROUPS - 1, g > 0)

    def y_start(i):
        for way in range(2):
            pl.when(sends[way])(y_copy(way, i).start)

    def f_start(i):
        for way in range(2):

            @pl.when(sends[1 - way])
            def _(way=way):
                y_copy(way, i).wait_recv()
                f_copy(way, i).start()

    def s_copy(i):
        return remote(part(i), cloud.at[1, core, i], s_send.at[i], s_recv.at[i], g, sib)

    def own_copy(i):
        src = pts_v if i == 0 else wts_v.at[pl.ds(F * (i - 1), F)]
        return pltpu.make_async_copy(src, cloud.at[1, core, i], own_sem.at[i])

    def x_at(d):
        return lax.rem(x + d, XS) * 2 + core

    def t_copy(d):
        return remote(pts, tgt.at[x], t_send.at[d], t_recv.at[d], g, x_at(d))

    def m_copy(d):
        return remote(meta, metas.at[x], m_send.at[d], m_recv.at[d], g, x_at(d))

    own_t = pltpu.make_async_copy(pts_v, tgt.at[x], own_sem.at[PARTS])
    own_m = pltpu.make_async_copy(meta, metas.at[x], own_sem.at[PARTS + 1])

    loads[0].wait()
    loads[1].wait()
    picks = skg_v[...] - h * COLS
    onehot = (lax.broadcasted_iota(jnp.int32, (COLS, SK), 0) == picks).astype(BF)
    own_pts = pts_v[...]
    first = own_pts.astype(BF)
    rest = own_pts - first.astype(F32)
    second, third = halves(rest)
    chosen = mul(first, onehot) + mul(second, onehot) + mul(third, onehot)
    ps_send[...] = chosen.reshape(HELP, PROWS, SK)

    pl.semaphore_wait(barrier, HELP + GROUPS - 2)

    def ps_copy(d):
        to = helper_at(d)
        return remote(ps_send.at[to], ps_buf.at[h], ps_ss.at[d], ps_rs.at[d], g, to)

    def us_copy(d):
        to = helper_at(d)
        return remote(us_send.at[to], us_buf.at[h], us_ss.at[d], us_rs.at[d], g, to)

    def lp_copy(d):
        return remote(lp_send, lp_buf.at[g], lp_ss.at[d], lp_rs.at[d], group_at(d), h)

    def lu_copy(d):
        return remote(lu_send, tier_u.at[g], lu_ss.at[d], lu_rs.at[d], group_at(d), h)

    def p_copy(d):
        return remote(lp_buf, p_buf.at[h], p_ss.at[d], p_rs.at[d], g, helper_at(d))

    def v_copy(d):
        return remote(v_buf.at[h], v_buf.at[h], v_ss.at[d], v_rs.at[d], g, helper_at(d))

    @pl.loop(1, HELP)
    def _(d):
        ps_copy(d).start()

    y_start(0)

    loads[2].wait()
    loads[3].wait()
    up = product3(wts_v[...], int_v[...].reshape(COLS, SK))
    us_send[...] = up.reshape(HELP, ROWS, SK)

    @pl.loop(1, HELP)
    def _(d):
        us_copy(d).start()

    y_start(1)

    @pl.loop(1, HELP)
    def _(d):
        ps_copy(d).wait_recv()

    ps_buf[h] = ps_send[h]
    total = ps_buf[0]
    for i in range(1, HELP):
        total = total + ps_buf[i]
    lp_send[...] = total
    lp_buf[g] = total

    @pl.loop(1, GROUPS)
    def _(d):
        lp_copy(d).start()

    @pl.loop(1, HELP)
    def _(d):
        us_copy(d).wait_recv()

    us_buf[h] = us_send[h]
    total = us_buf[0]
    for i in range(1, HELP):
        total = total + us_buf[i]
    lu_send[...] = total
    tier_u[g] = total

    @pl.loop(1, GROUPS)
    def _(d):
        lu_copy(d).start()

    y_start(2)

    @pl.loop(1, GROUPS)
    def _(d):
        lp_copy(d).wait_recv()

    @pl.loop(1, HELP)
    def _(d):
        p_copy(d).start()

    p_buf[h] = lp_buf[...]
    for d in range(1, XS):
        t_copy(d).start()
        m_copy(d).start()
    for i in range(PARTS):
        s_copy(i).start()
        own_copy(i).start()
    own_t.start()
    own_m.start()

    @pl.loop(1, GROUPS)
    def _(d):
        lu_copy(d).wait_recv()

    y_start(3)
    y_start(4)

    for copy in loads[4:]:
        copy.wait()

    @pl.loop(0, UPPER, unroll=2)
    def _(r):
        both = jnp.concatenate([tier_u[2 * r], tier_u[2 * r + 1]], axis=1)
        tier_u[GROUPS + r] = product3(both, tr[r])

    f_start(0)

    @pl.loop(1, HELP)
    def _(d):
        p_copy(d).wait_recv()

    @pl.loop(0, GROUPS)
    def _(n):
        tier_z[n] = stacked_halves(p_buf[:, n].reshape(F, SK)).astype(BF)

    rows = lax.broadcasted_iota(jnp.int32, (2 * SK, SK), 0)

    @pl.loop(0, UPPER, unroll=2)
    def _(r):
        both = jnp.concatenate([tier_z[2 * r], tier_z[2 * r + 1]], axis=1)
        pick = (rows == skn_v[pl.ds(r, 1), :]).astype(BF)
        tier_z[GROUPS + r] = mul(both, pick).astype(BF)

    f_start(1)
    sums = []
    for level in range(LEVELS):
        q = STARTS[level] + lax.shift_right_logical(g, level)
        right, target_own = target_side(tier_z[q].astype(F32))
        nodes = [STARTS[level] + far_s[q, slot] for slot in range(4)]
        both = jnp.concatenate([tier_z[node] for node in nodes], axis=1).astype(F32)
        left, source_own = source_side(both)
        block = jnp.exp2(mul(left, right) + source_own + target_own)
        values = jnp.concatenate([tier_u[node] for node in nodes], axis=1)
        sums.append(product3(values, block))

    f_start(2)
    local = sums[LEVELS - 1]
    for level in range(LEVELS - 1, 0, -1):
        r = STARTS[level] - GROUPS + lax.shift_right_logical(g, level)
        side = lax.rem(lax.shift_right_logical(g, level - 1), 2)
        half = tr[r, pl.ds(pl.multiple_of(side * SK, SK), SK), :]
        local = sums[level - 1] + product3(local, half, mul_t)
    v_buf[h] = local

    @pl.loop(1, HELP)
    def _(d):
        v_copy(d).start()

    f_start(3)
    f_start(4)

    @pl.loop(1, HELP)
    def _(d):
        v_copy(d).wait_recv()

    far_out[...] = product3(v_buf[...].reshape(R, SK), int_v[...].reshape(COLS, SK), mul_t)

    for i in range(PARTS):
        for way in range(2):
            pl.when(sends[1 - way])(f_copy(way, i).wait)
            pl.when(sends[way])(y_copy(way, i).wait_send)
        s_copy(i).wait()
        own_copy(i).wait()
    for d in range(1, XS):
        t_copy(d).wait()
        m_copy(d).wait()
    own_t.wait()
    own_m.wait()

    @pl.loop(1, HELP)
    def _(d):
        ps_copy(d).wait_send()
        us_copy(d).wait_send()
        p_copy(d).wait_send()
        v_copy(d).wait_send()

    @pl.loop(1, GROUPS)
    def _(d):
        lp_copy(d).wait_send()
        lu_copy(d).wait_send()


def spread(points, weights, interp, transfer, skel_group, skel_node, far_nodes, meta):
    vmem = pl.BlockSpec(memory_space=pltpu.VMEM)
    anym = pl.BlockSpec(memory_space=pl.ANY)
    dma = pltpu.SemaphoreType.DMA
    return pl.pallas_call(
        spread_kernel,
        out_shape=(
            jax.ShapeDtypeStruct((3, 2, PARTS, F, COLS), F32),
            jax.ShapeDtypeStruct((XS, F, COLS), F32),
            jax.ShapeDtypeStruct((XS, 8, 128), jnp.int32),
            jax.ShapeDtypeStruct((R, COLS), F32),
        ),
        in_specs=[anym] * 8,
        out_specs=(anym, anym, anym, vmem),
        scratch_shapes=[
            pltpu.VMEM((F, COLS), F32),
            pltpu.VMEM((R, COLS), F32),
            pltpu.VMEM((OWN, LEAF, SK), F32),
            pltpu.VMEM((UPPER, 2 * SK, SK), F32),
            pltpu.VMEM((1, SK), jnp.int32),
            pltpu.VMEM((UPPER, SK), jnp.int32),
            pltpu.SMEM((NODES, 4), jnp.int32),
            pltpu.VMEM((HELP, PROWS, SK), F32),
            pltpu.VMEM((HELP, PROWS, SK), F32),
            pltpu.VMEM((HELP, ROWS, SK), F32),
            pltpu.VMEM((HELP, ROWS, SK), F32),
            pltpu.VMEM((PROWS, SK), F32),
            pltpu.VMEM((GROUPS, PROWS, SK), F32),
            pltpu.VMEM((ROWS, SK), F32),
            pltpu.VMEM((HELP, GROUPS, PROWS, SK), F32),
            pltpu.VMEM((NODES, ROWS, SK), F32),
            pltpu.VMEM((NODES, 2 * F, SK), BF),
            pltpu.VMEM((HELP, ROWS, SK), F32),
            dma((7,)),
            dma((2, PARTS)), dma((2, PARTS)),
            dma((2, PARTS)), dma((2, PARTS)),
            dma((PARTS,)), dma((PARTS,)),
            dma((PARTS + 2,)),
            dma((XS,)), dma((XS,)),
            dma((XS,)), dma((XS,)),
            dma((HELP,)), dma((HELP,)),
            dma((HELP,)), dma((HELP,)),
            dma((GROUPS,)), dma((GROUPS,)),
            dma((GROUPS,)), dma((GROUPS,)),
            dma((HELP,)), dma((HELP,)),
            dma((HELP,)), dma((HELP,)),
        ],
        compiler_params=pltpu.CompilerParams(
            collective_id=0, has_side_effects=True, vmem_limit_bytes=60 << 20
        ),
        name="spread",
    )(points, weights, interp, transfer, skel_group, skel_node, far_nodes, meta)


SRC = 3 * 2 * OWN
TGT = XS * OWN
CUT = 2


def near_kernel(
    times, logs, cloud, tgt, part,
    w_hl, left, source_own, right, target_own,
    list_t, list_s, list_log, hi_a, lo_a, hi_b, lo_b,
):
    @pl.loop(0, 6)
    def _(pair):
        step, core = lax.div(pair, 2), lax.rem(pair, 2)
        for j in range(OWN):
            span = slice(j * LEAF, (j + 1) * LEAF)
            s = pair * OWN + j
            for i in range(R // F):
                high, low = halves(cloud[step, core, 1 + i, :, span])
                w_hl[s, i * F:(i + 1) * F, :] = high
                w_hl[s, R + i * F:R + (i + 1) * F, :] = low
            factor, own = source_side(stacked_halves(cloud[step, core, 0, :, span]))
            left[s] = factor
            source_own[s] = jnp.broadcast_to(own, (LEAF, 128))

    @pl.loop(0, XS)
    def _(at):
        for j in range(OWN):
            factor, own = target_side(stacked_halves(tgt[at, :, j * LEAF:(j + 1) * LEAF]))
            right[at * OWN + j] = factor
            target_own[at * OWN + j] = jnp.broadcast_to(own, (8, LEAF))
            part[at * OWN + j] = jnp.zeros((R, LEAF), F32)

    def note(k, n):
        list_t[n] = lax.div(k, SRC)
        list_s[n] = lax.rem(k, SRC)
        list_log[n] = logs[k]
        return n + (times[k] > 0).astype(jnp.int32)

    count = lax.fori_loop(0, TGT * SRC, note, jnp.int32(0))
    for extra in range(2):
        list_t[count + extra] = 0
        list_s[count + extra] = 0
        list_log[count + extra] = jnp.float32(-1e30)

    def produce(i, hi, lo):
        t, s = list_t[i], list_s[i]
        shift = target_own[t, 0:1, :] + list_log[i]
        own = source_own[s]
        for c in range(CUT):
            n = LEAF // CUT
            span = slice(c * n, (c + 1) * n)
            cross = mul(left[s], right[t, :, span])
            block = jnp.exp2(cross + jnp.concatenate([own] * (n // 128), axis=1) + shift[:, span])
            high, low = halves(block)
            hi[:, span] = high
            lo[:, span] = low

    def consume(i, hi, lo):
        t, s = list_t[i], list_s[i]
        for c in range(CUT):
            n = LEAF // CUT
            span = slice(c * n, (c + 1) * n)
            two = mul(w_hl[s], hi[:, span])
            part[t, :, span] += two[:R] + two[R:] + mul(w_hl[s, :R], lo[:, span])

    produce(0, hi_a, lo_a)

    @pl.loop(0, lax.div(count + 1, 2))
    def _(k):
        produce(2 * k + 1, hi_b, lo_b)
        consume(2 * k, hi_a, lo_a)
        produce(jnp.minimum(2 * k + 2, count), hi_a, lo_a)
        consume(2 * k + 1, hi_b, lo_b)


def near(times, logs, cloud, tgt):
    vmem = pl.BlockSpec(memory_space=pltpu.VMEM)
    smem = pl.BlockSpec(memory_space=pltpu.SMEM)
    return pl.pallas_call(
        near_kernel,
        out_shape=jax.ShapeDtypeStruct((TGT, R, LEAF), F32),
        in_specs=[smem, smem, vmem, vmem],
        out_specs=vmem,
        scratch_shapes=[
            pltpu.VMEM((SRC, 2 * R, LEAF), BF),
            pltpu.VMEM((SRC, LEAF, 4 * F), BF),
            pltpu.VMEM((SRC, LEAF, 128), F32),
            pltpu.VMEM((TGT, 4 * F, LEAF), BF),
            pltpu.VMEM((TGT, 8, LEAF), F32),
            pltpu.SMEM((TGT * SRC + 2,), jnp.int32),
            pltpu.SMEM((TGT * SRC + 2,), jnp.int32),
            pltpu.SMEM((TGT * SRC + 2,), F32),
            pltpu.VMEM((LEAF, LEAF), BF),
            pltpu.VMEM((LEAF, LEAF), BF),
            pltpu.VMEM((LEAF, LEAF), BF),
            pltpu.VMEM((LEAF, LEAF), BF),
        ],
        compiler_params=pltpu.CompilerParams(vmem_limit_bytes=48 << 20),
        name="near",
    )(times, logs, cloud, tgt)


def fold_kernel(part, far_out, out, first, last, first_ss, first_rs, last_ss, last_rs):
    g = lax.axis_index("leaf")
    h = lax.axis_index("help")
    x = lax.div(h, 2)
    core = lax.rem(h, 2)

    def x_at(d):
        return lax.rem(x + d, XS)

    def beside(way):
        return x_at(1 if way == 0 else 3)

    def to(way):
        return beside(way) * 2 + core

    barrier = pltpu.get_barrier_semaphore()
    for way in range(2):
        pl.semaphore_signal(barrier, inc=1, device_id=(g, to(way)), device_id_type=MESH)
    pl.semaphore_wait(barrier, 2)

    def first_copy(way):
        src = part.at[x_at(2) * OWN + way]
        return remote(src, first.at[way], first_ss.at[way], first_rs.at[way], g, to(way))

    def plain_copy(way):
        src = part.at[beside(way) * OWN + 1 - way]
        dst = last.at[way, 1 - way]
        return remote(src, dst, last_ss.at[way, 0], last_rs.at[way, 0], g, to(way))

    def sum_copy(way):
        dst = last.at[way, way]
        return remote(first.at[way], dst, last_ss.at[way, 1], last_rs.at[way, 1], g, to(way))

    for way in range(2):
        first_copy(way).start()
    for way in range(2):
        plain_copy(way).start()
    spans = [slice(j * LEAF, (j + 1) * LEAF) for j in range(OWN)]
    for j in range(OWN):
        out[:, spans[j]] = far_out[:, spans[j]] + part[x * OWN + j]
    for way in range(2):
        first_copy(way).wait_recv()
        first[way] += part[beside(way) * OWN + way]
        sum_copy(way).start()
    for way in range(2):
        plain_copy(way).wait_recv()
        out[:, spans[1 - way]] += last[way, 1 - way]
    for way in range(2):
        sum_copy(way).wait_recv()
        out[:, spans[way]] += last[way, way]
    for way in range(2):
        first_copy(way).wait_send()
        plain_copy(way).wait_send()
        sum_copy(way).wait_send()


def fold(part, far_out):
    vmem = pl.BlockSpec(memory_space=pltpu.VMEM)
    dma = pltpu.SemaphoreType.DMA
    return pl.pallas_call(
        fold_kernel,
        out_shape=jax.ShapeDtypeStruct((R, COLS), F32),
        in_specs=[vmem, vmem],
        out_specs=vmem,
        scratch_shapes=[
            pltpu.VMEM((2, R, LEAF), F32),
            pltpu.VMEM((2, OWN, R, LEAF), F32),
            dma((2,)), dma((2,)), dma((2, 2)), dma((2, 2)),
        ],
        compiler_params=pltpu.CompilerParams(
            collective_id=1, has_side_effects=True, vmem_limit_bytes=24 << 20
        ),
        name="fold",
    )(part, far_out)


def shards(
    points, weights, interp, transfer, near_count, near_src, skel_group, skel_node, far_nodes
):
    g = lax.axis_index("leaf")
    x = lax.axis_index("help") // 2
    listed = jnp.where(lax.iota(jnp.int32, NEAR)[None, :] < near_count[0][:, None], near_src, -1)
    meta = jnp.pad(listed, ((0, 8 - OWN), (0, 128 - NEAR)), constant_values=-1)
    cloud, tgt, metas, far_out = spread(
        points, weights, interp, transfer, skel_group, skel_node, far_nodes, meta
    )
    slots = metas[:, :OWN, :NEAR].reshape(TGT, 1, NEAR)
    step = lax.iota(jnp.int32, SRC)
    ids = (g - 1 + step // 4) * 16 + x * 4 + step % 4
    ids = jnp.where(ids < 0, -2, ids)
    times = jnp.sum((slots == ids[None, :, None]).astype(jnp.int32), axis=2).reshape(-1)
    logs = jnp.log2(jnp.maximum(times, 1).astype(F32))
    part = near(times, logs, cloud, tgt)
    return fold(part, far_out)


def solution(mesh):
    placed = (
        P(None, ("leaf", "help")),
        P(None, ("leaf", "help")),
        P(("leaf", "help"), None, None),
        P(),
        P("leaf", "help"),
        P(("leaf", "help"), None),
        P("leaf", None),
        P(),
        P(),
    )
    return jax.shard_map(
        shards, mesh=mesh, in_specs=placed, out_specs=P(None, ("leaf", "help")), check_vma=False
    )
```

time: 158 us -> 130 us (0.82)
  Pallas kernels: 146 us -> 123 us
  local copies, waits for them, and re-layouts: 9.79 us -> 5.14 us
    pallas_call x1, Pallas kernels: 79.9 us -> 61 us  [spread(): pl.pallas_call(spread_kernel, out_shape=(jax.ShapeDtypeStruct((3, 2, PART...]
    unnamed x14 -> x6, local copies, waits for them, and re-layouts: 9.62 us -> 3.58 us
    pallas_call x1, Pallas kernels: 28.9 us -> 23.1 us  [near(): pl.pallas_call(near_kernel, out_shape=jax.ShapeDtypeStruct((TGT, R, LEAF)...]
where the time goes in v2:
time: 130 us; the launch traced here: 129 us
  Pallas kernels  123 us (95%)
  local copies, waits for them, and re-layouts  5.14 us (4%)
    pallas_call x1, Pallas kernels, spread(): pl.pallas_call(spread_kernel, out_shape=(jax.ShapeDtypeStruct((3, 2, PART...  61 us
    pallas_call x1, Pallas kernels, fold(): pl.pallas_call(fold_kernel, out_shape=jax.ShapeDtypeStruct((R, COLS), F32...  38.5 us
    pallas_call x1, Pallas kernels, near(): pl.pallas_call(near_kernel, out_shape=jax.ShapeDtypeStruct((TGT, R, LEAF)...  23.1 us
    unnamed x6, local copies, waits for them, and re-layouts  3.58 us

profile of v2, /device:TPU:1, one launch (start us, length us, event | category | flops | bytes accessed | tf_op | source)
XLA Modules:
  0.0 128.9 jit_solution(12960543468948788033)
XLA Ops:
  0.0 0.8 compare_select_fusion.1
  0.8 0.6 pad.4.meta
  1.4 1.4 %copy.11.far = s32[30,4]{1,0:T(8,128)} copy(s32[30,4]{0,1:T(4,128)} %param.17) | data formatting | bytes 960 | tf_op args[8]
  2.7 61.0 %spread.1 = (f32[3,2,5,64,1024]{4,3,2,1,0:T(8,128)}, f32[4,64,1024]{2,1,0:T(8,128)}, s32[4,8,128]{2,1,0:T(8,128)}, f32[256,1024]{1,0:T(8,128)}) custom-call(f32[64,1024]{1,0:T(8,128)} %pts.1, f32[256,1024]{1,0:T(8,128)} %wts.1, f32[2,512,256]{2,1,0:T(8,128)} %interp.1, f32[14,512,256]{2,1,0:T(8,128)} %transfer.1, s32[1,256]{1,0:T(1,128)} %skg.1, ...), custom_call_target="tpu_custom_call" | custom-call | tf_op jit(solution)/shard_map/spread/pallas_call | solution.py:371
  63.8 0.0 copy-start
  63.8 0.8 slice.3
  64.6 0.3 convert_reduce_fusion
  64.9 0.1 copy.12
  65.0 0.1 reshape.32.times
  65.1 0.0 copy-start.1
  65.1 1.2 copy-done.1
  66.3 23.1 %near.1.part = f32[8,256,512]{2,1,0:T(8,128)S(1)} custom-call(s32[96]{0:T(128)S(1)} %reshape.32.times, f32[96]{0:T(128)S(1)} %log_multiply_fusion.logs, f32[3,2,5,64,1024]{4,3,2,1,0:T(8,128)} %get-tuple-element.10.cloud, f32[4,64,1024]{2,1,0:T(8,128)S(1)} %copy-done.1), custom_call_target="tpu_custom_call" | custom-call | tf_op jit(solution)/shard_map/near/pallas_call | solution.py:499
  89.4 0.0 copy-done
  89.4 38.5 %fold.1 = f32[256,1024]{1,0:T(8,128)S(1)} custom-call(f32[8,256,512]{2,1,0:T(8,128)S(1)} %near.1.part, f32[256,1024]{1,0:T(8,128)S(1)} %copy-done), custom_call_target="tpu_custom_call" | custom-call | tf_op jit(solution)/shard_map/fold/pallas_call | solution.py:582
  128.0 1.0 copy.14
  (2 shorter events, 0.0 us)
Async XLA Ops:
  63.8 25.7 %copy-start = (f32[256,1024]{1,0:T(8,128)S(1)}, f32[256,1024]{1,0:T(8,128)}, u32[]{:S(2)}) copy-start(f32[256,1024]{1,0:T(8,128)} %get-tuple-element.12.far_out) | copy-start | bytes 3145732
  65.1 1.2 copy-start.1

commit v3 on v2

--- a/solution.py
+++ b/solution.py
@@ -84,13 +84,13 @@
 
 
 def spread_kernel(
-    pts, wts, interp, transfer, skg, skn, far, meta,
-    cloud, tgt, metas, far_out,
-    pts_v, wts_v, int_v, tr, skg_v, skn_v, far_s,
-    ps_send, ps_buf, us_send, us_buf, lp_send, lp_buf, lu_send, p_buf, tier_u, tier_z, v_buf,
+    pts, wts, interp, transfer, skg, skn, meta,
+    cloud, tgt, metas, out_u, out_z,
+    pts_v, wts_v, int_v, tr, skg_v, skn_v,
+    ps_send, ps_buf, us_send, us_buf, lp_send, lp_buf, lu_send, p_buf, tier_u, tier_z,
     load_sem, y_send, y_recv, f_send, f_recv, s_send, s_recv, own_sem,
     t_send, t_recv, m_send, m_recv,
-    ps_ss, ps_rs, us_ss, us_rs, lp_ss, lp_rs, lu_ss, lu_rs, p_ss, p_rs, v_ss, v_rs,
+    ps_ss, ps_rs, us_ss, us_rs, lp_ss, lp_rs, lu_ss, lu_rs, p_ss, p_rs,
 ):
     g = lax.axis_index("leaf")
     h = lax.axis_index("help")
@@ -118,7 +118,7 @@
 
     pairs = (
         (pts, pts_v), (skg, skg_v), (wts, wts_v), (interp, int_v),
-        (far, far_s), (skn, skn_v), (transfer, tr),
+        (skn, skn_v), (transfer, tr),
     )
     loads = [
         pltpu.make_async_copy(src, dst, load_sem.at[i]) for i, (src, dst) in enumerate(pairs)
@@ -202,9 +202,6 @@
     def p_copy(d):
         return remote(lp_buf, p_buf.at[h], p_ss.at[d], p_rs.at[d], g, helper_at(d))
 
-    def v_copy(d):
-        return remote(v_buf.at[h], v_buf.at[h], v_ss.at[d], v_rs.at[d], g, helper_at(d))
-
     @pl.loop(1, HELP)
     def _(d):
         ps_copy(d).start()
@@ -253,6 +250,7 @@
         lu_copy(d).start()
 
     y_start(2)
+    y_start(3)
 
     @pl.loop(1, GROUPS)
     def _(d):
@@ -262,6 +260,7 @@
     def _(d):
         p_copy(d).start()
 
+    y_start(4)
     p_buf[h] = lp_buf[...]
     for d in range(1, XS):
         t_copy(d).start()
@@ -276,9 +275,6 @@
     def _(d):
         lu_copy(d).wait_recv()
 
-    y_start(3)
-    y_start(4)
-
     for copy in loads[4:]:
         copy.wait()
 
@@ -305,39 +301,14 @@
         pick = (rows == skn_v[pl.ds(r, 1), :]).astype(BF)
         tier_z[GROUPS + r] = mul(both, pick).astype(BF)
 
-    f_start(1)
-    sums = []
-    for level in range(LEVELS):
-        q = STARTS[level] + lax.shift_right_logical(g, level)
-        right, target_own = target_side(tier_z[q].astype(F32))
-        nodes = [STARTS[level] + far_s[q, slot] for slot in range(4)]
-        both = jnp.concatenate([tier_z[node] for node in nodes], axis=1).astype(F32)
-        left, source_own = source_side(both)
-        block = jnp.exp2(mul(left, right) + source_own + target_own)
-        values = jnp.concatenate([tier_u[node] for node in nodes], axis=1)
-        sums.append(product3(values, block))
-
-    f_start(2)
-    local = sums[LEVELS - 1]
-    for level in range(LEVELS - 1, 0, -1):
-        r = STARTS[level] - GROUPS + lax.shift_right_logical(g, level)
-        side = lax.rem(lax.shift_right_logical(g, level - 1), 2)
-        half = tr[r, pl.ds(pl.multiple_of(side * SK, SK), SK), :]
-        local = sums[level - 1] + product3(local, half, mul_t)
-    v_buf[h] = local
-
-    @pl.loop(1, HELP)
-    def _(d):
-        v_copy(d).start()
-
-    f_start(3)
-    f_start(4)
-
-    @pl.loop(1, HELP)
-    def _(d):
-        v_copy(d).wait_recv()
-
-    far_out[...] = product3(v_buf[...].reshape(R, SK), int_v[...].reshape(COLS, SK), mul_t)
+    tiers_out = (
+        pltpu.make_async_copy(tier_u, out_u, own_sem.at[PARTS + 2]),
+        pltpu.make_async_copy(tier_z, out_z, own_sem.at[PARTS + 3]),
+    )
+    for copy in tiers_out:
+        copy.start()
+    for i in range(1, PARTS):
+        f_start(i)
 
     for i in range(PARTS):
         for way in range(2):
@@ -350,13 +321,14 @@
         m_copy(d).wait()
     own_t.wait()
     own_m.wait()
+    for copy in tiers_out:
+        copy.wait()
 
     @pl.loop(1, HELP)
     def _(d):
         ps_copy(d).wait_send()
         us_copy(d).wait_send()
         p_copy(d).wait_send()
-        v_copy(d).wait_send()
 
     @pl.loop(1, GROUPS)
     def _(d):
@@ -364,8 +336,7 @@
         lu_copy(d).wait_send()
 
 
-def spread(points, weights, interp, transfer, skel_group, skel_node, far_nodes, meta):
-    vmem = pl.BlockSpec(memory_space=pltpu.VMEM)
+def spread(points, weights, interp, transfer, skel_group, skel_node, meta):
     anym = pl.BlockSpec(memory_space=pl.ANY)
     dma = pltpu.SemaphoreType.DMA
     return pl.pallas_call(
@@ -373,11 +344,12 @@
         out_shape=(
             jax.ShapeDtypeStruct((3, 2, PARTS, F, COLS), F32),
             jax.ShapeDtypeStruct((XS, F, COLS), F32),
-            jax.ShapeDtypeStruct((XS, 8, 128), jnp.int32),
-            jax.ShapeDtypeStruct((R, COLS), F32),
+            jax.ShapeDtypeStruct((XS, OWN, NEAR), jnp.int32),
+            jax.ShapeDtypeStruct((NODES, ROWS, SK), F32),
+            jax.ShapeDtypeStruct((NODES, 2 * F, SK), BF),
         ),
-        in_specs=[anym] * 8,
-        out_specs=(anym, anym, anym, vmem),
+        in_specs=[anym] * 7,
+        out_specs=(anym,) * 5,
         scratch_shapes=[
             pltpu.VMEM((F, COLS), F32),
             pltpu.VMEM((R, COLS), F32),
@@ -385,7 +357,6 @@
             pltpu.VMEM((UPPER, 2 * SK, SK), F32),
             pltpu.VMEM((1, SK), jnp.int32),
             pltpu.VMEM((UPPER, SK), jnp.int32),
-            pltpu.SMEM((NODES, 4), jnp.int32),
             pltpu.VMEM((HELP, PROWS, SK), F32),
             pltpu.VMEM((HELP, PROWS, SK), F32),
             pltpu.VMEM((HELP, ROWS, SK), F32),
@@ -396,12 +367,11 @@
             pltpu.VMEM((HELP, GROUPS, PROWS, SK), F32),
             pltpu.VMEM((NODES, ROWS, SK), F32),
             pltpu.VMEM((NODES, 2 * F, SK), BF),
-            pltpu.VMEM((HELP, ROWS, SK), F32),
-            dma((7,)),
+            dma((6,)),
             dma((2, PARTS)), dma((2, PARTS)),
             dma((2, PARTS)), dma((2, PARTS)),
             dma((PARTS,)), dma((PARTS,)),
-            dma((PARTS + 2,)),
+            dma((PARTS + 4,)),
             dma((XS,)), dma((XS,)),
             dma((XS,)), dma((XS,)),
             dma((HELP,)), dma((HELP,)),
@@ -409,13 +379,12 @@
             dma((GROUPS,)), dma((GROUPS,)),
             dma((GROUPS,)), dma((GROUPS,)),
             dma((HELP,)), dma((HELP,)),
-            dma((HELP,)), dma((HELP,)),
         ],
         compiler_params=pltpu.CompilerParams(
             collective_id=0, has_side_effects=True, vmem_limit_bytes=60 << 20
         ),
         name="spread",
-    )(points, weights, interp, transfer, skel_group, skel_node, far_nodes, meta)
+    )(points, weights, interp, transfer, skel_group, skel_node, meta)
 
 
 SRC = 3 * 2 * OWN
@@ -426,29 +395,38 @@
 def near_kernel(
     times, logs, cloud, tgt, part,
     w_hl, left, source_own, right, target_own,
-    list_t, list_s, list_log, hi_a, lo_a, hi_b, lo_b,
+    list_t, list_s, list_log, hi_a, lo_a, hi_b, lo_b, cloud_v, tgt_v, sems,
 ):
+    def cloud_copy(pair):
+        step, core = lax.div(pair, 2), lax.rem(pair, 2)
+        return pltpu.make_async_copy(cloud.at[step, core], cloud_v.at[pair], sems.at[pair])
+
+    tgt_copy = pltpu.make_async_copy(tgt, tgt_v, sems.at[6])
+    tgt_copy.start()
+    for pair in range(6):
+        cloud_copy(pair).start()
+    tgt_copy.wait()
+    @pl.loop(0, XS)
+    def _(at):
+        for j in range(OWN):
+            factor, own = target_side(stacked_halves(tgt_v[at, :, j * LEAF:(j + 1) * LEAF]))
+            right[at * OWN + j] = factor
+            target_own[at * OWN + j] = jnp.broadcast_to(own, (8, LEAF))
+            part[at * OWN + j] = jnp.zeros((R, LEAF), F32)
+
     @pl.loop(0, 6)
     def _(pair):
-        step, core = lax.div(pair, 2), lax.rem(pair, 2)
+        cloud_copy(pair).wait()
         for j in range(OWN):
             span = slice(j * LEAF, (j + 1) * LEAF)
             s = pair * OWN + j
             for i in range(R // F):
-                high, low = halves(cloud[step, core, 1 + i, :, span])
+                high, low = halves(cloud_v[pair, 1 + i, :, span])
                 w_hl[s, i * F:(i + 1) * F, :] = high
                 w_hl[s, R + i * F:R + (i + 1) * F, :] = low
-            factor, own = source_side(stacked_halves(cloud[step, core, 0, :, span]))
+            factor, own = source_side(stacked_halves(cloud_v[pair, 0, :, span]))
             left[s] = factor
             source_own[s] = jnp.broadcast_to(own, (LEAF, 128))
-
-    @pl.loop(0, XS)
-    def _(at):
-        for j in range(OWN):
-            factor, own = target_side(stacked_halves(tgt[at, :, j * LEAF:(j + 1) * LEAF]))
-            right[at * OWN + j] = factor
-            target_own[at * OWN + j] = jnp.broadcast_to(own, (8, LEAF))
-            part[at * OWN + j] = jnp.zeros((R, LEAF), F32)
 
     def note(k, n):
         list_t[n] = lax.div(k, SRC)
@@ -495,11 +473,12 @@
 
 def near(times, logs, cloud, tgt):
     vmem = pl.BlockSpec(memory_space=pltpu.VMEM)
+    anym = pl.BlockSpec(memory_space=pl.ANY)
     smem = pl.BlockSpec(memory_space=pltpu.SMEM)
     return pl.pallas_call(
         near_kernel,
         out_shape=jax.ShapeDtypeStruct((TGT, R, LEAF), F32),
-        in_specs=[smem, smem, vmem, vmem],
+        in_specs=[smem, smem, anym, anym],
         out_specs=vmem,
         scratch_shapes=[
             pltpu.VMEM((SRC, 2 * R, LEAF), BF),
@@ -514,18 +493,29 @@
             pltpu.VMEM((LEAF, LEAF), BF),
             pltpu.VMEM((LEAF, LEAF), BF),
             pltpu.VMEM((LEAF, LEAF), BF),
+            pltpu.VMEM((6, PARTS, F, COLS), F32),
+            pltpu.VMEM((XS, F, COLS), F32),
+            pltpu.SemaphoreType.DMA((7,)),
         ],
         compiler_params=pltpu.CompilerParams(vmem_limit_bytes=48 << 20),
         name="near",
     )(times, logs, cloud, tgt)
 
 
-def fold_kernel(part, far_out, out, first, last, first_ss, first_rs, last_ss, last_rs):
+def fold_kernel(
+    part, tier_u, tier_z, interp, transfer, far,
+    out,
+    first, last, u_v, z_v, int_v, half_v, far_s, v_buf,
+    load_sem, first_ss, first_rs, last_ss, last_rs, v_ss, v_rs,
+):
     g = lax.axis_index("leaf")
     h = lax.axis_index("help")
     x = lax.div(h, 2)
     core = lax.rem(h, 2)
 
+    def helper_at(d):
+        return lax.rem(h + d, HELP)
+
     def x_at(d):
         return lax.rem(x + d, XS)
 
@@ -536,9 +526,23 @@
         return beside(way) * 2 + core
 
     barrier = pltpu.get_barrier_semaphore()
-    for way in range(2):
-        pl.semaphore_signal(barrier, inc=1, device_id=(g, to(way)), device_id_type=MESH)
-    pl.semaphore_wait(barrier, 2)
+
+    @pl.loop(1, HELP)
+    def _(d):
+        pl.semaphore_signal(barrier, inc=1, device_id=(g, helper_at(d)), device_id_type=MESH)
+
+    pairs = [(far, far_s), (tier_z, z_v), (tier_u, u_v), (interp, int_v)]
+    for level in range(1, LEVELS):
+        r = STARTS[level] - GROUPS + lax.shift_right_logical(g, level)
+        side = lax.rem(lax.shift_right_logical(g, level - 1), 2)
+        rows = pl.ds(pl.multiple_of(side * SK, SK), SK)
+        pairs.append((transfer.at[r, rows], half_v.at[level - 1]))
+    loads = [
+        pltpu.make_async_copy(src, dst, load_sem.at[i]) for i, (src, dst) in enumerate(pairs)
+    ]
+    for copy in loads:
+        copy.start()
+    pl.semaphore_wait(barrier, HELP - 1)
 
     def first_copy(way):
         src = part.at[x_at(2) * OWN + way]
@@ -553,17 +557,48 @@
         dst = last.at[way, way]
         return remote(first.at[way], dst, last_ss.at[way, 1], last_rs.at[way, 1], g, to(way))
 
+    def v_copy(d):
+        return remote(v_buf.at[h], v_buf.at[h], v_ss.at[d], v_rs.at[d], g, helper_at(d))
+
     for way in range(2):
         first_copy(way).start()
     for way in range(2):
         plain_copy(way).start()
-    spans = [slice(j * LEAF, (j + 1) * LEAF) for j in range(OWN)]
-    for j in range(OWN):
-        out[:, spans[j]] = far_out[:, spans[j]] + part[x * OWN + j]
+
+    for copy in loads:
+        copy.wait()
+    sums = []
+    for level in range(LEVELS):
+        q = STARTS[level] + lax.shift_right_logical(g, level)
+        right, target_own = target_side(z_v[q].astype(F32))
+        nodes = [STARTS[level] + far_s[slot, q] for slot in range(4)]
+        both = jnp.concatenate([z_v[node] for node in nodes], axis=1).astype(F32)
+        left, source_own = source_side(both)
+        block = jnp.exp2(mul(left, right) + source_own + target_own)
+        values = jnp.concatenate([u_v[node] for node in nodes], axis=1)
+        sums.append(product3(values, block))
+    local = sums[LEVELS - 1]
+    for level in range(LEVELS - 1, 0, -1):
+        local = sums[level - 1] + product3(local, half_v[level - 1], mul_t)
+    v_buf[h] = local
+
+    @pl.loop(1, HELP)
+    def _(d):
+        v_copy(d).start()
+
     for way in range(2):
         first_copy(way).wait_recv()
         first[way] += part[beside(way) * OWN + way]
         sum_copy(way).start()
+
+    @pl.loop(1, HELP)
+    def _(d):
+        v_copy(d).wait_recv()
+
+    values = v_buf[...].reshape(R, SK)
+    spans = [slice(j * LEAF, (j + 1) * LEAF) for j in range(OWN)]
+    for j in range(OWN):
+        out[:, spans[j]] = part[x * OWN + j] + product3(values, int_v[j], mul_t)
     for way in range(2):
         plain_copy(way).wait_recv()
         out[:, spans[1 - way]] += last[way, 1 - way]
@@ -575,25 +610,37 @@
         plain_copy(way).wait_send()
         sum_copy(way).wait_send()
 
-
-def fold(part, far_out):
+    @pl.loop(1, HELP)
+    def _(d):
+        v_copy(d).wait_send()
+
+
+def fold(part, tier_u, tier_z, interp, transfer, far_slots):
     vmem = pl.BlockSpec(memory_space=pltpu.VMEM)
+    anym = pl.BlockSpec(memory_space=pl.ANY)
     dma = pltpu.SemaphoreType.DMA
     return pl.pallas_call(
         fold_kernel,
         out_shape=jax.ShapeDtypeStruct((R, COLS), F32),
-        in_specs=[vmem, vmem],
+        in_specs=[vmem] + [anym] * 5,
         out_specs=vmem,
         scratch_shapes=[
             pltpu.VMEM((2, R, LEAF), F32),
             pltpu.VMEM((2, OWN, R, LEAF), F32),
-            dma((2,)), dma((2,)), dma((2, 2)), dma((2, 2)),
+            pltpu.VMEM((NODES, ROWS, SK), F32),
+            pltpu.VMEM((NODES, 2 * F, SK), BF),
+            pltpu.VMEM((OWN, LEAF, SK), F32),
+            pltpu.VMEM((LEVELS - 1, SK, SK), F32),
+            pltpu.SMEM((4, NODES), jnp.int32),
+            pltpu.VMEM((HELP, ROWS, SK), F32),
+            dma((7,)),
+            dma((2,)), dma((2,)), dma((2, 2)), dma((2, 2)), dma((HELP,)), dma((HELP,)),
         ],
         compiler_params=pltpu.CompilerParams(
-            collective_id=1, has_side_effects=True, vmem_limit_bytes=24 << 20
+            collective_id=1, has_side_effects=True, vmem_limit_bytes=32 << 20
         ),
         name="fold",
-    )(part, far_out)
+    )(part, tier_u, tier_z, interp, transfer, far_slots)
 
 
 def shards(
@@ -602,18 +649,17 @@
     g = lax.axis_index("leaf")
     x = lax.axis_index("help") // 2
     listed = jnp.where(lax.iota(jnp.int32, NEAR)[None, :] < near_count[0][:, None], near_src, -1)
-    meta = jnp.pad(listed, ((0, 8 - OWN), (0, 128 - NEAR)), constant_values=-1)
-    cloud, tgt, metas, far_out = spread(
-        points, weights, interp, transfer, skel_group, skel_node, far_nodes, meta
+    cloud, tgt, metas, tier_u, tier_z = spread(
+        points, weights, interp, transfer, skel_group, skel_node, listed
     )
-    slots = metas[:, :OWN, :NEAR].reshape(TGT, 1, NEAR)
+    slots = metas.reshape(TGT, 1, NEAR)
     step = lax.iota(jnp.int32, SRC)
     ids = (g - 1 + step // 4) * 16 + x * 4 + step % 4
     ids = jnp.where(ids < 0, -2, ids)
     times = jnp.sum((slots == ids[None, :, None]).astype(jnp.int32), axis=2).reshape(-1)
     logs = jnp.log2(jnp.maximum(times, 1).astype(F32))
     part = near(times, logs, cloud, tgt)
-    return fold(part, far_out)
+    return fold(part, tier_u, tier_z, interp, transfer, far_nodes.T)
 
 
 def solution(mesh):

time: 130 us -> 130 us (level)
  local copies, waits for them, and re-layouts: 5.14 us -> 3.72 us
    pallas_call x1, Pallas kernels: 61 us -> 55.6 us  [spread(): pl.pallas_call(spread_kernel, out_shape=(jax.ShapeDtypeStruct((3, 2, PART...]
    pallas_call x1, Pallas kernels: 38.5 us -> 41.2 us  [fold(): pl.pallas_call(fold_kernel, out_shape=jax.ShapeDtypeStruct((R, COLS), F32...]
    pallas_call x1, Pallas kernels: 23.1 us -> 25.6 us  [near(): pl.pallas_call(near_kernel, out_shape=jax.ShapeDtypeStruct((TGT, R, LEAF)...]
    unnamed x6 -> x15, local copies, waits for them, and re-layouts: 3.58 us -> 3.56 us
where the time goes in v3:
time: 130 us; the launch traced here: 129 us
  Pallas kernels  122 us (94%)
  local copies, waits for them, and re-layouts  3.72 us (3%)
  other arithmetic  2.36 us (2%)
    pallas_call x1, Pallas kernels, spread(): pl.pallas_call(spread_kernel, out_shape=(jax.ShapeDtypeStruct((3, 2, PART...  55.6 us
    pallas_call x1, Pallas kernels, fold(): pl.pallas_call(fold_kernel, out_shape=jax.ShapeDtypeStruct((R, COLS), F32...  41.2 us
    pallas_call x1, Pallas kernels, near(): pl.pallas_call(near_kernel, out_shape=jax.ShapeDtypeStruct((TGT, R, LEAF)...  25.6 us
    unnamed x15, local copies, waits for them, and re-layouts  3.56 us

profile of v3, /device:TPU:1, one launch (start us, length us, event | category | flops | bytes accessed | tf_op | source)
XLA Modules:
  0.0 128.6 jit_solution(12406822207575887181)
XLA Ops:
  0.0 1.3 %compare_select_fusion.1.meta = s32[2,32]{1,0:T(2,128)} fusion(s32[2,32]{1,0:T(2,128)} %param.14, s32[2]{0:T(128)} %bitcast.7), kind=kLoop, calls=%fused_computation.4 | loop fusion | flops 128 | bytes 520 | tf_op jit(solution)/shard_map/jit(_where)/select_n | solution.py:651
  1.3 0.0 slice-start
  1.3 55.6 %spread.1 = (f32[3,2,5,64,1024]{4,3,2,1,0:T(8,128)}, f32[4,64,1024]{2,1,0:T(8,128)}, s32[4,2,32]{2,1,0:T(2,128)}, f32[30,32,256]{2,1,0:T(8,128)}, bf16[30,128,256]{2,1,0:T(8,128)(2,1)}) custom-call(f32[64,1024]{1,0:T(8,128)} %pts.1, f32[256,1024]{1,0:T(8,128)} %wts.1, f32[2,512,256]{2,1,0:T(8,128)} %interp.3, f32[14,512,256]{2,1,0:T(8,128)} %transfer.3, ...), custom_call_target="tpu_custom_call" | custom-call | tf_op jit(solution)/shard_map/spread/pallas_call | solution.py:342
  57.0 0.0 copy-start.4
  57.0 1.0 convert_reduce_fusion
  58.0 0.1 copy.10
  58.1 0.1 reshape.32.times
  58.2 0.0 copy-start
  58.2 0.0 copy-start.1
  58.2 0.0 copy-start.2
  58.2 1.4 %copy-done.2 = f32[4,64,1024]{2,1,0:T(8,128)S(1)} copy-done((f32[4,64,1024]{2,1,0:T(8,128)S(1)}, f32[4,64,1024]{2,1,0:T(8,128)}, u32[]{:S(2)}) %copy-start.2) | copy-done | bytes 1048600
  59.6 0.0 slice-start.1
  59.6 25.6 %near.1.part = f32[8,256,512]{2,1,0:T(8,128)S(1)} custom-call(s32[96]{0:T(128)S(1)} %reshape.32.times, f32[96]{0:T(128)S(1)} %log_multiply_fusion.logs, f32[3,2,5,64,1024]{4,3,2,1,0:T(8,128)} %get-tuple-element.11.cloud, f32[4,64,1024]{2,1,0:T(8,128)S(1)} %copy-done.2), custom_call_target="tpu_custom_call" | custom-call | tf_op jit(solution)/shard_map/near/pallas_call | solution.py:478
  85.2 0.0 slice-done
  85.2 0.0 copy-done.4
  85.2 0.0 copy-done
  85.2 0.0 copy-done.1
  85.3 0.0 slice-done.1
  85.3 0.0 copy-start.3
  85.3 1.2 copy-done.3
  86.5 41.2 %fold.1 = f32[256,1024]{1,0:T(8,128)S(1)} custom-call(f32[8,256,512]{2,1,0:T(8,128)S(1)} %near.1.part, f32[30,32,256]{2,1,0:T(8,128)S(1)} %copy-done.3, bf16[30,128,256]{2,1,0:T(8,128)(2,1)S(1)} %copy-done.1, f32[2,512,256]{2,1,0:T(8,128)S(1)} %copy-done, f32[14,512,256]{2,1,0:T(8,128)S(1)} %bitcast.4, s32[4,30]{1,0:T(4,128)S(1)} %bitcast.5), custom_call_target="tpu_custom_call" | custom-call | tf_op jit(solution)/shard_map/fold/pallas_call | solution.py:622
  127.7 1.0 copy.12
  (3 shorter events, 0.0 us)
Async XLA Ops:
  1.3 83.9 %slice-start = ((s8[7340032]{0:T(1024)(128)(4,1)}), s8[3145728]{0:T(1024)(128)(4,1)S(1)}, s32[]{:S(2)}) async-start(s8[7340032]{0:T(1024)(128)(4,1)} %bitcast.3), calls=%async_computation | async-start | bytes 6291456
  57.0 28.3 %copy-start.4 = (s32[30,4]{0,1:T(4,128)S(1)}, s32[30,4]{0,1:T(4,128)}, u32[]{:S(2)}) copy-start(s32[30,4]{0,1:T(4,128)} %param.17) | copy-start | bytes 1444
  58.2 27.1 %copy-start = (f32[2,512,256]{2,1,0:T(8,128)S(1)}, f32[2,512,256]{2,1,0:T(8,128)}, u32[]{:S(2)}) copy-start(f32[2,512,256]{2,1,0:T(8,128)} %interp.3) | copy-start | bytes 3145732
  58.2 27.1 %copy-start.1 = (bf16[30,128,256]{2,1,0:T(8,128)(2,1)S(1)}, bf16[30,128,256]{2,1,0:T(8,128)(2,1)}, u32[]{:S(2)}) copy-start(bf16[30,128,256]{2,1,0:T(8,128)(2,1)} %get-tuple-element.14.tier_z) | copy-start | bytes 5898244
  58.2 1.4 %copy-start.2 = (f32[4,64,1024]{2,1,0:T(8,128)S(1)}, f32[4,64,1024]{2,1,0:T(8,128)}, u32[]{:S(2)}) copy-start(f32[4,64,1024]{2,1,0:T(8,128)} %get-tuple-element.12.tgt) | copy-start | bytes 3145732
  59.6 25.7 %slice-start.1 = ((s8[7340032]{0:T(1024)(128)(4,1)}), s8[4194304]{0:T(1024)(128)(4,1)S(1)}, s32[]{:S(2)}) async-start(s8[7340032]{0:T(1024)(128)(4,1)} %bitcast.3), calls=%async_computation.1 | async-start | bytes 8388608
  85.3 1.2 copy-start.3

commit v4 on v3

--- a/solution.py
+++ b/solution.py
@@ -84,9 +84,9 @@
 
 
 def spread_kernel(
-    pts, wts, interp, transfer, skg, skn, meta,
-    cloud, tgt, metas, out_u, out_z,
-    pts_v, wts_v, int_v, tr, skg_v, skn_v,
+    pts, wts, interp, transfer, skg, skn, far, meta,
+    cloud, tgt, metas, own_v,
+    pts_v, wts_v, int_v, tr, skg_v, skn_v, far_s,
     ps_send, ps_buf, us_send, us_buf, lp_send, lp_buf, lu_send, p_buf, tier_u, tier_z,
     load_sem, y_send, y_recv, f_send, f_recv, s_send, s_recv, own_sem,
     t_send, t_recv, m_send, m_recv,
@@ -118,7 +118,7 @@
 
     pairs = (
         (pts, pts_v), (skg, skg_v), (wts, wts_v), (interp, int_v),
-        (skn, skn_v), (transfer, tr),
+        (skn, skn_v), (transfer, tr), (far, far_s),
     )
     loads = [
         pltpu.make_async_copy(src, dst, load_sem.at[i]) for i, (src, dst) in enumerate(pairs)
@@ -183,41 +183,50 @@
     chosen = mul(first, onehot) + mul(second, onehot) + mul(third, onehot)
     ps_send[...] = chosen.reshape(HELP, PROWS, SK)
 
-    pl.semaphore_wait(barrier, HELP + GROUPS - 2)
-
-    def ps_copy(d):
-        to = helper_at(d)
-        return remote(ps_send.at[to], ps_buf.at[h], ps_ss.at[d], ps_rs.at[d], g, to)
-
-    def us_copy(d):
-        to = helper_at(d)
-        return remote(us_send.at[to], us_buf.at[h], us_ss.at[d], us_rs.at[d], g, to)
-
-    def lp_copy(d):
-        return remote(lp_send, lp_buf.at[g], lp_ss.at[d], lp_rs.at[d], group_at(d), h)
-
-    def lu_copy(d):
-        return remote(lu_send, tier_u.at[g], lu_ss.at[d], lu_rs.at[d], group_at(d), h)
-
-    def p_copy(d):
-        return remote(lp_buf, p_buf.at[h], p_ss.at[d], p_rs.at[d], g, helper_at(d))
-
-    @pl.loop(1, HELP)
-    def _(d):
-        ps_copy(d).start()
-
-    y_start(0)
-
     loads[2].wait()
     loads[3].wait()
     up = product3(wts_v[...], int_v[...].reshape(COLS, SK))
     us_send[...] = up.reshape(HELP, ROWS, SK)
 
+    pl.semaphore_wait(barrier, HELP + GROUPS - 2)
+
+    def ps_copy(d):
+        to = helper_at(d)
+        return remote(ps_send.at[to], ps_buf.at[h], ps_ss.at[d], ps_rs.at[d], g, to)
+
+    def us_copy(d):
+        to = helper_at(d)
+        return remote(us_send.at[to], us_buf.at[h], us_ss.at[d], us_rs.at[d], g, to)
+
+    def lp_copy(d):
+        return remote(lp_send, lp_buf.at[g], lp_ss.at[d], lp_rs.at[d], group_at(d), h)
+
+    def lu_copy(d):
+        return remote(lu_send, tier_u.at[g], lu_ss.at[d], lu_rs.at[d], group_at(d), h)
+
+    def p_copy(d):
+        return remote(lp_buf, p_buf.at[h], p_ss.at[d], p_rs.at[d], g, helper_at(d))
+
     @pl.loop(1, HELP)
     def _(d):
         us_copy(d).start()
-
-    y_start(1)
+        ps_copy(d).start()
+
+    y_start(0)
+    @pl.loop(1, HELP)
+    def _(d):
+        us_copy(d).wait_recv()
+
+    us_buf[h] = us_send[h]
+    total = us_buf[0]
+    for i in range(1, HELP):
+        total = total + us_buf[i]
+    lu_send[...] = total
+    tier_u[g] = total
+
+    @pl.loop(1, GROUPS)
+    def _(d):
+        lu_copy(d).start()
 
     @pl.loop(1, HELP)
     def _(d):
@@ -234,34 +243,18 @@
     def _(d):
         lp_copy(d).start()
 
-    @pl.loop(1, HELP)
-    def _(d):
-        us_copy(d).wait_recv()
-
-    us_buf[h] = us_send[h]
-    total = us_buf[0]
-    for i in range(1, HELP):
-        total = total + us_buf[i]
-    lu_send[...] = total
-    tier_u[g] = total
+    y_start(1)
+    y_start(2)
 
     @pl.loop(1, GROUPS)
     def _(d):
-        lu_copy(d).start()
-
-    y_start(2)
+        lp_copy(d).wait_recv()
+
+    @pl.loop(1, HELP)
+    def _(d):
+        p_copy(d).start()
+
     y_start(3)
-
-    @pl.loop(1, GROUPS)
-    def _(d):
-        lp_copy(d).wait_recv()
-
-    @pl.loop(1, HELP)
-    def _(d):
-        p_copy(d).start()
-
-    y_start(4)
-    p_buf[h] = lp_buf[...]
     for d in range(1, XS):
         t_copy(d).start()
         m_copy(d).start()
@@ -270,10 +263,13 @@
         own_copy(i).start()
     own_t.start()
     own_m.start()
+    p_buf[h] = lp_buf[...]
 
     @pl.loop(1, GROUPS)
     def _(d):
         lu_copy(d).wait_recv()
+
+    y_start(4)
 
     for copy in loads[4:]:
         copy.wait()
@@ -301,13 +297,26 @@
         pick = (rows == skn_v[pl.ds(r, 1), :]).astype(BF)
         tier_z[GROUPS + r] = mul(both, pick).astype(BF)
 
-    tiers_out = (
-        pltpu.make_async_copy(tier_u, out_u, own_sem.at[PARTS + 2]),
-        pltpu.make_async_copy(tier_z, out_z, own_sem.at[PARTS + 3]),
-    )
-    for copy in tiers_out:
-        copy.start()
-    for i in range(1, PARTS):
+    f_start(1)
+    sums = []
+    for level in range(LEVELS):
+        q = STARTS[level] + lax.shift_right_logical(g, level)
+        right, target_own = target_side(tier_z[q].astype(F32))
+        nodes = [STARTS[level] + far_s[slot, q] for slot in range(4)]
+        both = jnp.concatenate([tier_z[node] for node in nodes], axis=1).astype(F32)
+        left, source_own = source_side(both)
+        block = jnp.exp2(mul(left, right) + source_own + target_own)
+        values = jnp.concatenate([tier_u[node] for node in nodes], axis=1)
+        sums.append(product3(values, block))
+    f_start(2)
+    local = sums[LEVELS - 1]
+    for level in range(LEVELS - 1, 0, -1):
+        r = STARTS[level] - GROUPS + lax.shift_right_logical(g, level)
+        side = lax.rem(lax.shift_right_logical(g, level - 1), 2)
+        half = tr[r, pl.ds(pl.multiple_of(side * SK, SK), SK), :]
+        local = sums[level - 1] + product3(local, half, mul_t)
+    own_v[...] = local
+    for i in range(3, PARTS):
         f_start(i)
 
     for i in range(PARTS):
@@ -321,8 +330,6 @@
         m_copy(d).wait()
     own_t.wait()
     own_m.wait()
-    for copy in tiers_out:
-        copy.wait()
 
     @pl.loop(1, HELP)
     def _(d):
@@ -336,7 +343,8 @@
         lu_copy(d).wait_send()
 
 
-def spread(points, weights, interp, transfer, skel_group, skel_node, meta):
+def spread(points, weights, interp, transfer, skel_group, skel_node, far_slots, meta):
+    vmem = pl.BlockSpec(memory_space=pltpu.VMEM)
     anym = pl.BlockSpec(memory_space=pl.ANY)
     dma = pltpu.SemaphoreType.DMA
     return pl.pallas_call(
@@ -345,11 +353,10 @@
             jax.ShapeDtypeStruct((3, 2, PARTS, F, COLS), F32),
             jax.ShapeDtypeStruct((XS, F, COLS), F32),
             jax.ShapeDtypeStruct((XS, OWN, NEAR), jnp.int32),
-            jax.ShapeDtypeStruct((NODES, ROWS, SK), F32),
-            jax.ShapeDtypeStruct((NODES, 2 * F, SK), BF),
+            jax.ShapeDtypeStruct((ROWS, SK), F32),
         ),
-        in_specs=[anym] * 7,
-        out_specs=(anym,) * 5,
+        in_specs=[anym] * 8,
+        out_specs=(anym, anym, anym, vmem),
         scratch_shapes=[
             pltpu.VMEM((F, COLS), F32),
             pltpu.VMEM((R, COLS), F32),
@@ -357,6 +364,7 @@
             pltpu.VMEM((UPPER, 2 * SK, SK), F32),
             pltpu.VMEM((1, SK), jnp.int32),
             pltpu.VMEM((UPPER, SK), jnp.int32),
+            pltpu.SMEM((4, NODES), jnp.int32),
             pltpu.VMEM((HELP, PROWS, SK), F32),
             pltpu.VMEM((HELP, PROWS, SK), F32),
             pltpu.VMEM((HELP, ROWS, SK), F32),
@@ -367,11 +375,11 @@
             pltpu.VMEM((HELP, GROUPS, PROWS, SK), F32),
             pltpu.VMEM((NODES, ROWS, SK), F32),
             pltpu.VMEM((NODES, 2 * F, SK), BF),
-            dma((6,)),
+            dma((7,)),
             dma((2, PARTS)), dma((2, PARTS)),
             dma((2, PARTS)), dma((2, PARTS)),
             dma((PARTS,)), dma((PARTS,)),
-            dma((PARTS + 4,)),
+            dma((PARTS + 2,)),
             dma((XS,)), dma((XS,)),
             dma((XS,)), dma((XS,)),
             dma((HELP,)), dma((HELP,)),
@@ -384,7 +392,7 @@
             collective_id=0, has_side_effects=True, vmem_limit_bytes=60 << 20
         ),
         name="spread",
-    )(points, weights, interp, transfer, skel_group, skel_node, meta)
+    )(points, weights, interp, transfer, skel_group, skel_node, far_slots, meta)
 
 
 SRC = 3 * 2 * OWN
@@ -503,9 +511,9 @@
 
 
 def fold_kernel(
-    part, tier_u, tier_z, interp, transfer, far,
+    part, own_v, interp,
     out,
-    first, last, u_v, z_v, int_v, half_v, far_s, v_buf,
+    first, last, int_v, v_buf,
     load_sem, first_ss, first_rs, last_ss, last_rs, v_ss, v_rs,
 ):
     g = lax.axis_index("leaf")
@@ -531,17 +539,8 @@
     def _(d):
         pl.semaphore_signal(barrier, inc=1, device_id=(g, helper_at(d)), device_id_type=MESH)
 
-    pairs = [(far, far_s), (tier_z, z_v), (tier_u, u_v), (interp, int_v)]
-    for level in range(1, LEVELS):
-        r = STARTS[level] - GROUPS + lax.shift_right_logical(g, level)
-        side = lax.rem(lax.shift_right_logical(g, level - 1), 2)
-        rows = pl.ds(pl.multiple_of(side * SK, SK), SK)
-        pairs.append((transfer.at[r, rows], half_v.at[level - 1]))
-    loads = [
-        pltpu.make_async_copy(src, dst, load_sem.at[i]) for i, (src, dst) in enumerate(pairs)
-    ]
-    for copy in loads:
-        copy.start()
+    load = pltpu.make_async_copy(interp, int_v, load_sem)
+    load.start()
     pl.semaphore_wait(barrier, HELP - 1)
 
     def first_copy(way):
@@ -558,33 +557,18 @@
         return remote(first.at[way], dst, last_ss.at[way, 1], last_rs.at[way, 1], g, to(way))
 
     def v_copy(d):
-        return remote(v_buf.at[h], v_buf.at[h], v_ss.at[d], v_rs.at[d], g, helper_at(d))
+        return remote(own_v, v_buf.at[h], v_ss.at[d], v_rs.at[d], g, helper_at(d))
+
+    @pl.loop(1, HELP)
+    def _(d):
+        v_copy(d).start()
 
     for way in range(2):
         first_copy(way).start()
     for way in range(2):
         plain_copy(way).start()
-
-    for copy in loads:
-        copy.wait()
-    sums = []
-    for level in range(LEVELS):
-        q = STARTS[level] + lax.shift_right_logical(g, level)
-        right, target_own = target_side(z_v[q].astype(F32))
-        nodes = [STARTS[level] + far_s[slot, q] for slot in range(4)]
-        both = jnp.concatenate([z_v[node] for node in nodes], axis=1).astype(F32)
-        left, source_own = source_side(both)
-        block = jnp.exp2(mul(left, right) + source_own + target_own)
-        values = jnp.concatenate([u_v[node] for node in nodes], axis=1)
-        sums.append(product3(values, block))
-    local = sums[LEVELS - 1]
-    for level in range(LEVELS - 1, 0, -1):
-        local = sums[level - 1] + product3(local, half_v[level - 1], mul_t)
-    v_buf[h] = local
-
-    @pl.loop(1, HELP)
-    def _(d):
-        v_copy(d).start()
+    v_buf[h] = own_v[...]
+    load.wait()
 
     for way in range(2):
         first_copy(way).wait_recv()
@@ -615,32 +599,28 @@
         v_copy(d).wait_send()
 
 
-def fold(part, tier_u, tier_z, interp, transfer, far_slots):
+def fold(part, own_v, interp):
     vmem = pl.BlockSpec(memory_space=pltpu.VMEM)
     anym = pl.BlockSpec(memory_space=pl.ANY)
     dma = pltpu.SemaphoreType.DMA
     return pl.pallas_call(
         fold_kernel,
         out_shape=jax.ShapeDtypeStruct((R, COLS), F32),
-        in_specs=[vmem] + [anym] * 5,
+        in_specs=[vmem, vmem, anym],
         out_specs=vmem,
         scratch_shapes=[
             pltpu.VMEM((2, R, LEAF), F32),
             pltpu.VMEM((2, OWN, R, LEAF), F32),
-            pltpu.VMEM((NODES, ROWS, SK), F32),
-            pltpu.VMEM((NODES, 2 * F, SK), BF),
             pltpu.VMEM((OWN, LEAF, SK), F32),
-            pltpu.VMEM((LEVELS - 1, SK, SK), F32),
-            pltpu.SMEM((4, NODES), jnp.int32),
             pltpu.VMEM((HELP, ROWS, SK), F32),
-            dma((7,)),
+            dma,
             dma((2,)), dma((2,)), dma((2, 2)), dma((2, 2)), dma((HELP,)), dma((HELP,)),
         ],
         compiler_params=pltpu.CompilerParams(
             collective_id=1, has_side_effects=True, vmem_limit_bytes=32 << 20
         ),
         name="fold",
-    )(part, tier_u, tier_z, interp, transfer, far_slots)
+    )(part, own_v, interp)
 
 
 def shards(
@@ -649,8 +629,8 @@
     g = lax.axis_index("leaf")
     x = lax.axis_index("help") // 2
     listed = jnp.where(lax.iota(jnp.int32, NEAR)[None, :] < near_count[0][:, None], near_src, -1)
-    cloud, tgt, metas, tier_u, tier_z = spread(
-        points, weights, interp, transfer, skel_group, skel_node, listed
+    cloud, tgt, metas, own_v = spread(
+        points, weights, interp, transfer, skel_group, skel_node, far_nodes.T, listed
     )
     slots = metas.reshape(TGT, 1, NEAR)
     step = lax.iota(jnp.int32, SRC)
@@ -659,7 +639,7 @@
     times = jnp.sum((slots == ids[None, :, None]).astype(jnp.int32), axis=2).reshape(-1)
     logs = jnp.log2(jnp.maximum(times, 1).astype(F32))
     part = near(times, logs, cloud, tgt)
-    return fold(part, tier_u, tier_z, interp, transfer, far_nodes.T)
+    return fold(part, own_v, interp)
 
 
 def solution(mesh):

time: 130 us -> 127 us (0.977)
  the two profiles are of different devices: /device:TPU:1 before, /device:TPU:24 now
where the time goes in v4:
time: 127 us
  Pallas kernels  122 us (96%)
  other arithmetic  2.45 us (2%)
  local copies, waits for them, and re-layouts  2.37 us (2%)
    pallas_call x1, Pallas kernels, spread(): pl.pallas_call(spread_kernel, out_shape=(jax.ShapeDtypeStruct((3, 2, PART...  50.8 us
    pallas_call x1, Pallas kernels, fold(): pl.pallas_call(fold_kernel, out_shape=jax.ShapeDtypeStruct((R, COLS), F32...  50.2 us
    pallas_call x1, Pallas kernels, near(): pl.pallas_call(near_kernel, out_shape=jax.ShapeDtypeStruct((TGT, R, LEAF)...  21.4 us

profile of v4, /device:TPU:24, one launch (start us, length us, event | category | flops | bytes accessed | tf_op | source)
XLA Modules:
  0.0 127.3 jit_solution(2421207389057119273)
XLA Ops:
  0.0 1.3 %compare_select_fusion.1.meta = s32[2,32]{1,0:T(2,128)} fusion(s32[2,32]{1,0:T(2,128)} %param.14, s32[2]{0:T(128)} %bitcast.5), kind=kLoop, calls=%fused_computation.4 | loop fusion | flops 128 | bytes 520 | tf_op jit(solution)/shard_map/jit(_where)/select_n | solution.py:631
  1.3 50.8 %spread.1 = (f32[3,2,5,64,1024]{4,3,2,1,0:T(8,128)}, f32[4,64,1024]{2,1,0:T(8,128)}, s32[4,2,32]{2,1,0:T(2,128)}, f32[32,256]{1,0:T(8,128)}) custom-call(f32[64,1024]{1,0:T(8,128)} %pts.1, f32[256,1024]{1,0:T(8,128)} %wts.1, f32[2,512,256]{2,1,0:T(8,128)} %interp.3, f32[14,512,256]{2,1,0:T(8,128)} %transfer.1, s32[1,256]{1,0:T(1,128)} %skg.1, ...), custom_call_target="tpu_custom_call" | custom-call | tf_op jit(solution)/shard_map/spread/pallas_call | solution.py:350
  52.1 0.0 copy-start
  52.1 1.1 convert_reduce_fusion
  53.2 0.1 copy.10
  53.3 0.1 reshape.32.times
  53.4 0.0 copy-start.1
  53.4 1.2 copy-done.1
  54.6 0.0 copy-start.2
  54.6 21.4 %near.1.part = f32[8,256,512]{2,1,0:T(8,128)S(1)} custom-call(s32[96]{0:T(128)S(1)} %reshape.32.times, f32[96]{0:T(128)S(1)} %log_multiply_fusion.logs, f32[3,2,5,64,1024]{4,3,2,1,0:T(8,128)} %get-tuple-element.10.cloud, f32[4,64,1024]{2,1,0:T(8,128)S(1)} %copy-done.1), custom_call_target="tpu_custom_call" | custom-call | tf_op jit(solution)/shard_map/near/pallas_call | solution.py:486
  76.1 0.0 copy-done
  76.1 0.0 copy-done.2
  76.1 50.2 %fold.1 = f32[256,1024]{1,0:T(8,128)S(1)} custom-call(f32[8,256,512]{2,1,0:T(8,128)S(1)} %near.1.part, f32[32,256]{1,0:T(8,128)S(1)} %copy-done.2, f32[2,512,256]{2,1,0:T(8,128)S(1)} %copy-done), custom_call_target="tpu_custom_call" | custom-call | tf_op jit(solution)/shard_map/fold/pallas_call | solution.py:606
  126.3 1.0 copy.12
  (2 shorter events, 0.0 us)
Async XLA Ops:
  52.1 24.0 %copy-start = (f32[2,512,256]{2,1,0:T(8,128)S(1)}, f32[2,512,256]{2,1,0:T(8,128)}, u32[]{:S(2)}) copy-start(f32[2,512,256]{2,1,0:T(8,128)} %interp.3) | copy-start | bytes 3145732
  53.4 1.2 copy-start.1
  54.6 21.5 %copy-start.2 = (f32[32,256]{1,0:T(8,128)S(1)}, f32[32,256]{1,0:T(8,128)}, u32[]{:S(2)}) copy-start(f32[32,256]{1,0:T(8,128)} %get-tuple-element.12.own_v) | copy-start | bytes 98308

commit v5 on v4

--- a/solution.py
+++ b/solution.py
@@ -85,12 +85,12 @@
 
 def spread_kernel(
     pts, wts, interp, transfer, skg, skn, far, meta,
-    cloud, tgt, metas, own_v,
+    cloud, tgt, metas, v_out,
     pts_v, wts_v, int_v, tr, skg_v, skn_v, far_s,
-    ps_send, ps_buf, us_send, us_buf, lp_send, lp_buf, lu_send, p_buf, tier_u, tier_z,
+    ps_send, ps_buf, us_send, us_buf, lp_send, lp_buf, lu_send, p_buf, tier_u, tier_z, v_buf,
     load_sem, y_send, y_recv, f_send, f_recv, s_send, s_recv, own_sem,
     t_send, t_recv, m_send, m_recv,
-    ps_ss, ps_rs, us_ss, us_rs, lp_ss, lp_rs, lu_ss, lu_rs, p_ss, p_rs,
+    ps_ss, ps_rs, us_ss, us_rs, lp_ss, lp_rs, lu_ss, lu_rs, p_ss, p_rs, v_ss, v_rs,
 ):
     g = lax.axis_index("leaf")
     h = lax.axis_index("help")
@@ -206,6 +206,9 @@
 
     def p_copy(d):
         return remote(lp_buf, p_buf.at[h], p_ss.at[d], p_rs.at[d], g, helper_at(d))
+
+    def v_copy(d):
+        return remote(v_buf.at[h], v_buf.at[h], v_ss.at[d], v_rs.at[d], g, helper_at(d))
 
     @pl.loop(1, HELP)
     def _(d):
@@ -315,9 +318,20 @@
         side = lax.rem(lax.shift_right_logical(g, level - 1), 2)
         half = tr[r, pl.ds(pl.multiple_of(side * SK, SK), SK), :]
         local = sums[level - 1] + product3(local, half, mul_t)
-    own_v[...] = local
+    v_buf[h] = local
+
+    @pl.loop(1, HELP)
+    def _(d):
+        v_copy(d).start()
+
     for i in range(3, PARTS):
         f_start(i)
+
+    @pl.loop(1, HELP)
+    def _(d):
+        v_copy(d).wait_recv()
+
+    v_out[...] = v_buf[...].reshape(R, SK)
 
     for i in range(PARTS):
         for way in range(2):
@@ -336,6 +350,7 @@
         ps_copy(d).wait_send()
         us_copy(d).wait_send()
         p_copy(d).wait_send()
+        v_copy(d).wait_send()
 
     @pl.loop(1, GROUPS)
     def _(d):
@@ -353,7 +368,7 @@
             jax.ShapeDtypeStruct((3, 2, PARTS, F, COLS), F32),
             jax.ShapeDtypeStruct((XS, F, COLS), F32),
             jax.ShapeDtypeStruct((XS, OWN, NEAR), jnp.int32),
-            jax.ShapeDtypeStruct((ROWS, SK), F32),
+            jax.ShapeDtypeStruct((R, SK), F32),
         ),
         in_specs=[anym] * 8,
         out_specs=(anym, anym, anym, vmem),
@@ -375,6 +390,7 @@
             pltpu.VMEM((HELP, GROUPS, PROWS, SK), F32),
             pltpu.VMEM((NODES, ROWS, SK), F32),
             pltpu.VMEM((NODES, 2 * F, SK), BF),
+            pltpu.VMEM((HELP, ROWS, SK), F32),
             dma((7,)),
             dma((2, PARTS)), dma((2, PARTS)),
             dma((2, PARTS)), dma((2, PARTS)),
@@ -386,6 +402,7 @@
             dma((HELP,)), dma((HELP,)),
             dma((GROUPS,)), dma((GROUPS,)),
             dma((GROUPS,)), dma((GROUPS,)),
+            dma((HELP,)), dma((HELP,)),
             dma((HELP,)), dma((HELP,)),
         ],
         compiler_params=pltpu.CompilerParams(
@@ -511,19 +528,16 @@
 
 
 def fold_kernel(
-    part, own_v, interp,
+    part, values, interp,
     out,
-    first, last, int_v, v_buf,
-    load_sem, first_ss, first_rs, last_ss, last_rs, v_ss, v_rs,
+    first, last, int_v,
+    load_sem, first_ss, first_rs, last_ss, last_rs,
 ):
     g = lax.axis_index("leaf")
     h = lax.axis_index("help")
     x = lax.div(h, 2)
     core = lax.rem(h, 2)
 
-    def helper_at(d):
-        return lax.rem(h + d, HELP)
-
     def x_at(d):
         return lax.rem(x + d, XS)
 
@@ -535,13 +549,12 @@
 
     barrier = pltpu.get_barrier_semaphore()
 
-    @pl.loop(1, HELP)
-    def _(d):
-        pl.semaphore_signal(barrier, inc=1, device_id=(g, helper_at(d)), device_id_type=MESH)
+    for way in range(2):
+        pl.semaphore_signal(barrier, inc=1, device_id=(g, to(way)), device_id_type=MESH)
 
     load = pltpu.make_async_copy(interp, int_v, load_sem)
     load.start()
-    pl.semaphore_wait(barrier, HELP - 1)
+    pl.semaphore_wait(barrier, 2)
 
     def first_copy(way):
         src = part.at[x_at(2) * OWN + way]
@@ -556,33 +569,19 @@
         dst = last.at[way, way]
         return remote(first.at[way], dst, last_ss.at[way, 1], last_rs.at[way, 1], g, to(way))
 
-    def v_copy(d):
-        return remote(own_v, v_buf.at[h], v_ss.at[d], v_rs.at[d], g, helper_at(d))
-
-    @pl.loop(1, HELP)
-    def _(d):
-        v_copy(d).start()
-
     for way in range(2):
         first_copy(way).start()
     for way in range(2):
         plain_copy(way).start()
-    v_buf[h] = own_v[...]
     load.wait()
-
+    spans = [slice(j * LEAF, (j + 1) * LEAF) for j in range(OWN)]
+    for j in range(OWN):
+        out[:, spans[j]] = part[x * OWN + j] + product3(values[...], int_v[j], mul_t)
     for way in range(2):
         first_copy(way).wait_recv()
         first[way] += part[beside(way) * OWN + way]
         sum_copy(way).start()
 
-    @pl.loop(1, HELP)
-    def _(d):
-        v_copy(d).wait_recv()
-
-    values = v_buf[...].reshape(R, SK)
-    spans = [slice(j * LEAF, (j + 1) * LEAF) for j in range(OWN)]
-    for j in range(OWN):
-        out[:, spans[j]] = part[x * OWN + j] + product3(values, int_v[j], mul_t)
     for way in range(2):
         plain_copy(way).wait_recv()
         out[:, spans[1 - way]] += last[way, 1 - way]
@@ -594,12 +593,8 @@
         plain_copy(way).wait_send()
         sum_copy(way).wait_send()
 
-    @pl.loop(1, HELP)
-    def _(d):
-        v_copy(d).wait_send()
-
-
-def fold(part, own_v, interp):
+
+def fold(part, values, interp):
     vmem = pl.BlockSpec(memory_space=pltpu.VMEM)
     anym = pl.BlockSpec(memory_space=pl.ANY)
     dma = pltpu.SemaphoreType.DMA
@@ -612,15 +607,14 @@
             pltpu.VMEM((2, R, LEAF), F32),
             pltpu.VMEM((2, OWN, R, LEAF), F32),
             pltpu.VMEM((OWN, LEAF, SK), F32),
-            pltpu.VMEM((HELP, ROWS, SK), F32),
             dma,
-            dma((2,)), dma((2,)), dma((2, 2)), dma((2, 2)), dma((HELP,)), dma((HELP,)),
+            dma((2,)), dma((2,)), dma((2, 2)), dma((2, 2)),
         ],
         compiler_params=pltpu.CompilerParams(
             collective_id=1, has_side_effects=True, vmem_limit_bytes=32 << 20
         ),
         name="fold",
-    )(part, own_v, interp)
+    )(part, values, interp)
 
 
 def shards(
@@ -629,7 +623,7 @@
     g = lax.axis_index("leaf")
     x = lax.axis_index("help") // 2
     listed = jnp.where(lax.iota(jnp.int32, NEAR)[None, :] < near_count[0][:, None], near_src, -1)
-    cloud, tgt, metas, own_v = spread(
+    cloud, tgt, metas, values = spread(
         points, weights, interp, transfer, skel_group, skel_node, far_nodes.T, listed
     )
     slots = metas.reshape(TGT, 1, NEAR)
@@ -639,7 +633,7 @@
     times = jnp.sum((slots == ids[None, :, None]).astype(jnp.int32), axis=2).reshape(-1)
     logs = jnp.log2(jnp.maximum(times, 1).astype(F32))
     part = near(times, logs, cloud, tgt)
-    return fold(part, own_v, interp)
+    return fold(part, values, interp)
 
 
 def solution(mesh):

time: 127 us -> 125 us (0.984)
  the two profiles are of different devices: /device:TPU:24 before, /device:TPU:1 now
where the time goes in v5:
time: 125 us; the launch traced here: 122 us
  Pallas kernels  117 us (94%)
  other arithmetic  2.44 us (2%)
  local copies, waits for them, and re-layouts  2.37 us (2%)
    pallas_call x1, Pallas kernels, spread(): pl.pallas_call(spread_kernel, out_shape=(jax.ShapeDtypeStruct((3, 2, PART...  56 us
    pallas_call x1, Pallas kernels, fold(): pl.pallas_call(fold_kernel, out_shape=jax.ShapeDtypeStruct((R, COLS), F32...  37.3 us
    pallas_call x1, Pallas kernels, near(): pl.pallas_call(near_kernel, out_shape=jax.ShapeDtypeStruct((TGT, R, LEAF)...  24.1 us

profile of v5, /device:TPU:1, one launch (start us, length us, event | category | flops | bytes accessed | tf_op | source)
XLA Modules:
  0.0 122.2 jit_solution(11716452355280487844)
XLA Ops:
  0.0 1.3 %compare_select_fusion.1.meta = s32[2,32]{1,0:T(2,128)} fusion(s32[2,32]{1,0:T(2,128)} %param.14, s32[2]{0:T(128)} %bitcast.5), kind=kLoop, calls=%fused_computation.4 | loop fusion | flops 128 | bytes 520 | tf_op jit(solution)/shard_map/jit(_where)/select_n | solution.py:625
  1.3 56.0 %spread.1 = (f32[3,2,5,64,1024]{4,3,2,1,0:T(8,128)}, f32[4,64,1024]{2,1,0:T(8,128)}, s32[4,2,32]{2,1,0:T(2,128)}, f32[256,256]{1,0:T(8,128)}) custom-call(f32[64,1024]{1,0:T(8,128)} %pts.1, f32[256,1024]{1,0:T(8,128)} %wts.1, f32[2,512,256]{2,1,0:T(8,128)} %interp.3, f32[14,512,256]{2,1,0:T(8,128)} %transfer.1, s32[1,256]{1,0:T(1,128)} %skg.1, ...), custom_call_target="tpu_custom_call" | custom-call | tf_op jit(solution)/shard_map/spread/pallas_call | solution.py:365
  57.3 0.0 copy-start
  57.3 1.1 convert_reduce_fusion
  58.4 0.1 copy.10
  58.5 0.1 reshape.32.times
  58.6 0.0 copy-start.1
  58.6 1.2 %copy-done.1 = f32[4,64,1024]{2,1,0:T(8,128)S(1)} copy-done((f32[4,64,1024]{2,1,0:T(8,128)S(1)}, f32[4,64,1024]{2,1,0:T(8,128)}, u32[]{:S(2)}) %copy-start.1) | copy-done | bytes 1048600
  59.8 0.0 copy-start.2
  59.8 24.1 %near.1.part = f32[8,256,512]{2,1,0:T(8,128)S(1)} custom-call(s32[96]{0:T(128)S(1)} %reshape.32.times, f32[96]{0:T(128)S(1)} %log_multiply_fusion.logs, f32[3,2,5,64,1024]{4,3,2,1,0:T(8,128)} %get-tuple-element.10.cloud, f32[4,64,1024]{2,1,0:T(8,128)S(1)} %copy-done.1), custom_call_target="tpu_custom_call" | custom-call | tf_op jit(solution)/shard_map/near/pallas_call | solution.py:503
  83.9 0.0 copy-done
  83.9 0.0 copy-done.2
  83.9 37.3 %fold.1 = f32[256,1024]{1,0:T(8,128)S(1)} custom-call(f32[8,256,512]{2,1,0:T(8,128)S(1)} %near.1.part, f32[256,256]{1,0:T(8,128)S(1)} %copy-done.2, f32[2,512,256]{2,1,0:T(8,128)S(1)} %copy-done), custom_call_target="tpu_custom_call" | custom-call | tf_op jit(solution)/shard_map/fold/pallas_call | solution.py:601
  121.2 1.0 copy.12
  (2 shorter events, 0.0 us)
Async XLA Ops:
  57.3 26.6 %copy-start = (f32[2,512,256]{2,1,0:T(8,128)S(1)}, f32[2,512,256]{2,1,0:T(8,128)}, u32[]{:S(2)}) copy-start(f32[2,512,256]{2,1,0:T(8,128)} %interp.3) | copy-start | bytes 3145732
  58.6 1.2 %copy-start.1 = (f32[4,64,1024]{2,1,0:T(8,128)S(1)}, f32[4,64,1024]{2,1,0:T(8,128)}, u32[]{:S(2)}) copy-start(f32[4,64,1024]{2,1,0:T(8,128)} %get-tuple-element.11.tgt) | copy-start | bytes 3145732
  59.8 24.1 %copy-start.2 = (f32[256,256]{1,0:T(8,128)S(1)}, f32[256,256]{1,0:T(8,128)}, u32[]{:S(2)}) copy-start(f32[256,256]{1,0:T(8,128)} %get-tuple-element.12.values) | copy-start | bytes 786436

commit v6 on v5

--- a/solution.py
+++ b/solution.py
@@ -246,18 +246,6 @@
     def _(d):
         lp_copy(d).start()
 
-    y_start(1)
-    y_start(2)
-
-    @pl.loop(1, GROUPS)
-    def _(d):
-        lp_copy(d).wait_recv()
-
-    @pl.loop(1, HELP)
-    def _(d):
-        p_copy(d).start()
-
-    y_start(3)
     for d in range(1, XS):
         t_copy(d).start()
         m_copy(d).start()
@@ -266,6 +254,18 @@
         own_copy(i).start()
     own_t.start()
     own_m.start()
+    y_start(1)
+    y_start(2)
+
+    @pl.loop(1, GROUPS)
+    def _(d):
+        lp_copy(d).wait_recv()
+
+    @pl.loop(1, HELP)
+    def _(d):
+        p_copy(d).start()
+
+    y_start(3)
     p_buf[h] = lp_buf[...]
 
     @pl.loop(1, GROUPS)
@@ -434,9 +434,9 @@
     @pl.loop(0, XS)
     def _(at):
         for j in range(OWN):
-            factor, own = target_side(stacked_halves(tgt_v[at, :, j * LEAF:(j + 1) * LEAF]))
+            factor, own = source_side(stacked_halves(tgt_v[at, :, j * LEAF:(j + 1) * LEAF]))
             right[at * OWN + j] = factor
-            target_own[at * OWN + j] = jnp.broadcast_to(own, (8, LEAF))
+            target_own[at * OWN + j] = jnp.broadcast_to(own, (LEAF, 128))
             part[at * OWN + j] = jnp.zeros((R, LEAF), F32)
 
     @pl.loop(0, 6)
@@ -449,9 +449,9 @@
                 high, low = halves(cloud_v[pair, 1 + i, :, span])
                 w_hl[s, i * F:(i + 1) * F, :] = high
                 w_hl[s, R + i * F:R + (i + 1) * F, :] = low
-            factor, own = source_side(stacked_halves(cloud_v[pair, 0, :, span]))
+            factor, own = target_side(stacked_halves(cloud_v[pair, 0, :, span]))
             left[s] = factor
-            source_own[s] = jnp.broadcast_to(own, (LEAF, 128))
+            source_own[s] = jnp.broadcast_to(own, (8, LEAF))
 
     def note(k, n):
         list_t[n] = lax.div(k, SRC)
@@ -467,24 +467,24 @@
 
     def produce(i, hi, lo):
         t, s = list_t[i], list_s[i]
-        shift = target_own[t, 0:1, :] + list_log[i]
-        own = source_own[s]
+        shift = source_own[s, 0:1, :] + list_log[i]
         for c in range(CUT):
             n = LEAF // CUT
             span = slice(c * n, (c + 1) * n)
-            cross = mul(left[s], right[t, :, span])
-            block = jnp.exp2(cross + jnp.concatenate([own] * (n // 128), axis=1) + shift[:, span])
+            cross = mul(right[t, span], left[s])
+            own = target_own[t, span]
+            block = jnp.exp2(cross + jnp.concatenate([own] * 4, axis=1) + shift)
             high, low = halves(block)
-            hi[:, span] = high
-            lo[:, span] = low
+            hi[span] = high
+            lo[span] = low
 
     def consume(i, hi, lo):
         t, s = list_t[i], list_s[i]
         for c in range(CUT):
             n = LEAF // CUT
             span = slice(c * n, (c + 1) * n)
-            two = mul(w_hl[s], hi[:, span])
-            part[t, :, span] += two[:R] + two[R:] + mul(w_hl[s, :R], lo[:, span])
+            two = mul_t(w_hl[s], hi[span])
+            part[t, :, span] += two[:R] + two[R:] + mul_t(w_hl[s, :R], lo[span])
 
     produce(0, hi_a, lo_a)
 
@@ -507,10 +507,10 @@
         out_specs=vmem,
         scratch_shapes=[
             pltpu.VMEM((SRC, 2 * R, LEAF), BF),
-            pltpu.VMEM((SRC, LEAF, 4 * F), BF),
-            pltpu.VMEM((SRC, LEAF, 128), F32),
-            pltpu.VMEM((TGT, 4 * F, LEAF), BF),
-            pltpu.VMEM((TGT, 8, LEAF), F32),
+            pltpu.VMEM((SRC, 4 * F, LEAF), BF),
+            pltpu.VMEM((SRC, 8, LEAF), F32),
+            pltpu.VMEM((TGT, LEAF, 4 * F), BF),
+            pltpu.VMEM((TGT, LEAF, 128), F32),
             pltpu.SMEM((TGT * SRC + 2,), jnp.int32),
             pltpu.SMEM((TGT * SRC + 2,), jnp.int32),
             pltpu.SMEM((TGT * SRC + 2,), F32),
@@ -528,9 +528,10 @@
 
 
 def fold_kernel(
-    part, values, interp,
+    logs, part, values, interp, cloud, pts,
     out,
-    first, last, int_v,
+    first, last, int_v, cloud_v, pts_v,
+    w_hl, left, source_own, right, target_own, hi, lo,
     load_sem, first_ss, first_rs, last_ss, last_rs,
 ):
     g = lax.axis_index("leaf")
@@ -552,8 +553,16 @@
     for way in range(2):
         pl.semaphore_signal(barrier, inc=1, device_id=(g, to(way)), device_id_type=MESH)
 
-    load = pltpu.make_async_copy(interp, int_v, load_sem)
-    load.start()
+    def cloud_copy(pair):
+        step, at = lax.div(pair, 2), lax.rem(pair, 2)
+        return pltpu.make_async_copy(cloud.at[step, at], cloud_v.at[pair], load_sem.at[pair])
+
+    pts_load = pltpu.make_async_copy(pts, pts_v, load_sem.at[6])
+    int_load = pltpu.make_async_copy(interp, int_v, load_sem.at[7])
+    pts_load.start()
+    for pair in range(6):
+        cloud_copy(pair).start()
+    int_load.start()
     pl.semaphore_wait(barrier, 2)
 
     def first_copy(way):
@@ -573,14 +582,58 @@
         first_copy(way).start()
     for way in range(2):
         plain_copy(way).start()
-    load.wait()
+
     spans = [slice(j * LEAF, (j + 1) * LEAF) for j in range(OWN)]
+    pts_load.wait()
+    for t in range(OWN):
+        factor, own = source_side(stacked_halves(pts_v[:, spans[t]]))
+        right[t] = factor
+        target_own[t] = jnp.broadcast_to(own, (LEAF, 128))
+    int_load.wait()
     for j in range(OWN):
-        out[:, spans[j]] = part[x * OWN + j] + product3(values[...], int_v[j], mul_t)
+        out[:, spans[j]] = product3(values[...], int_v[j], mul_t)
+
+    def tiles(pair):
+        cloud_copy(pair).wait()
+        step = lax.div(pair, 2)
+        missing = ((step == 0) & (g == 0)) | ((step == 2) & (g == GROUPS - 1))
+        for j in range(OWN):
+            for i in range(R // F):
+                value = jnp.where(missing, 0.0, cloud_v[pair, 1 + i, :, spans[j]])
+                high, low = halves(value)
+                w_hl[j, i * F:(i + 1) * F, :] = high
+                w_hl[j, R + i * F:R + (i + 1) * F, :] = low
+            value = jnp.where(missing, 0.0, cloud_v[pair, 0, :, spans[j]])
+            factor, own = target_side(stacked_halves(value))
+            left[j] = factor
+            source_own[j] = jnp.broadcast_to(own, (8, LEAF))
+        for j in range(OWN):
+            for t in range(OWN):
+                shift = source_own[j, 0:1, :] + logs[t * SRC + pair * OWN + j]
+                for c in range(CUT):
+                    n = LEAF // CUT
+                    span = slice(c * n, (c + 1) * n)
+                    cross = mul(right[t, span], left[j])
+                    own = target_own[t, span]
+                    block = jnp.exp2(cross + jnp.concatenate([own] * 4, axis=1) + shift)
+                    high, low = halves(block)
+                    hi[j, t, span] = high
+                    lo[j, t, span] = low
+        for j in range(OWN):
+            for t in range(OWN):
+                for c in range(CUT):
+                    n = LEAF // CUT
+                    span = slice(c * n, (c + 1) * n)
+                    where = slice(t * LEAF + c * n, t * LEAF + (c + 1) * n)
+                    two = mul_t(w_hl[j], hi[j, t, span])
+                    out[:, where] += two[:R] + two[R:] + mul_t(w_hl[j, :R], lo[j, t, span])
+
+    pl.loop(0, 3)(tiles)
     for way in range(2):
         first_copy(way).wait_recv()
         first[way] += part[beside(way) * OWN + way]
         sum_copy(way).start()
+    pl.loop(3, 6)(tiles)
 
     for way in range(2):
         plain_copy(way).wait_recv()
@@ -594,27 +647,37 @@
         sum_copy(way).wait_send()
 
 
-def fold(part, values, interp):
+def fold(logs, part, values, interp, cloud, points):
     vmem = pl.BlockSpec(memory_space=pltpu.VMEM)
+    smem = pl.BlockSpec(memory_space=pltpu.SMEM)
     anym = pl.BlockSpec(memory_space=pl.ANY)
     dma = pltpu.SemaphoreType.DMA
     return pl.pallas_call(
         fold_kernel,
         out_shape=jax.ShapeDtypeStruct((R, COLS), F32),
-        in_specs=[vmem, vmem, anym],
+        in_specs=[smem, vmem, vmem, anym, anym, anym],
         out_specs=vmem,
         scratch_shapes=[
             pltpu.VMEM((2, R, LEAF), F32),
             pltpu.VMEM((2, OWN, R, LEAF), F32),
             pltpu.VMEM((OWN, LEAF, SK), F32),
-            dma,
+            pltpu.VMEM((6, PARTS, F, COLS), F32),
+            pltpu.VMEM((F, COLS), F32),
+            pltpu.VMEM((OWN, 2 * R, LEAF), BF),
+            pltpu.VMEM((OWN, 4 * F, LEAF), BF),
+            pltpu.VMEM((OWN, 8, LEAF), F32),
+            pltpu.VMEM((OWN, LEAF, 4 * F), BF),
+            pltpu.VMEM((OWN, LEAF, 128), F32),
+            pltpu.VMEM((OWN, OWN, LEAF, LEAF), BF),
+            pltpu.VMEM((OWN, OWN, LEAF, LEAF), BF),
+            dma((8,)),
             dma((2,)), dma((2,)), dma((2, 2)), dma((2, 2)),
         ],
         compiler_params=pltpu.CompilerParams(
-            collective_id=1, has_side_effects=True, vmem_limit_bytes=32 << 20
+            collective_id=1, has_side_effects=True, vmem_limit_bytes=44 << 20
         ),
         name="fold",
-    )(part, values, interp)
+    )(logs, part, values, interp, cloud, points)
 
 
 def shards(
@@ -630,10 +693,13 @@
     step = lax.iota(jnp.int32, SRC)
     ids = (g - 1 + step // 4) * 16 + x * 4 + step % 4
     ids = jnp.where(ids < 0, -2, ids)
-    times = jnp.sum((slots == ids[None, :, None]).astype(jnp.int32), axis=2).reshape(-1)
+    times = jnp.sum((slots == ids[None, :, None]).astype(jnp.int32), axis=2)
     logs = jnp.log2(jnp.maximum(times, 1).astype(F32))
-    part = near(times, logs, cloud, tgt)
-    return fold(part, values, interp)
+    own_logs = jnp.where(times > 0, logs, -1e30)
+    own_logs = lax.dynamic_slice_in_dim(own_logs, x * OWN, OWN, 0).reshape(-1)
+    away = lax.iota(jnp.int32, TGT)[:, None] // OWN != x
+    part = near(jnp.where(away, times, 0).reshape(-1), logs.reshape(-1), cloud, tgt)
+    return fold(own_logs, part, values, interp, cloud, points)
 
 
 def solution(mesh):

time: 125 us -> 117 us (0.936); the launches traced: 122 us -> 117 us
  Pallas kernels: 117 us -> 111 us
    pallas_call x1, Pallas kernels: 24.1 us -> 18.8 us  [near(): pl.pallas_call(near_kernel, out_shape=jax.ShapeDtypeStruct((TGT, R, LEAF)...]
where the time goes in v6:
time: 117 us
  Pallas kernels  111 us (95%)
  local copies, waits for them, and re-layouts  2.72 us (2%)
  other arithmetic  2.55 us (2%)
    pallas_call x1, Pallas kernels, spread(): pl.pallas_call(spread_kernel, out_shape=(jax.ShapeDtypeStruct((3, 2, PART...  54.8 us
    pallas_call x1, Pallas kernels, fold(): pl.pallas_call(fold_kernel, out_shape=jax.ShapeDtypeStruct((R, COLS), F32...  37.7 us
    pallas_call x1, Pallas kernels, near(): pl.pallas_call(near_kernel, out_shape=jax.ShapeDtypeStruct((TGT, R, LEAF)...  18.8 us

profile of v6, /device:TPU:1, one launch (start us, length us, event | category | flops | bytes accessed | tf_op | source)
XLA Modules:
  0.0 116.7 jit_solution(5289023588426016610)
XLA Ops:
  0.0 1.3 %compare_select_fusion.1.meta = s32[2,32]{1,0:T(2,128)} fusion(s32[2,32]{1,0:T(2,128)} %param.14, s32[2]{0:T(128)} %bitcast.5), kind=kLoop, calls=%fused_computation.9 | loop fusion | flops 128 | bytes 520 | tf_op jit(solution)/shard_map/jit(_where)/select_n | solution.py:688
  1.3 54.8 %spread.1 = (f32[3,2,5,64,1024]{4,3,2,1,0:T(8,128)}, f32[4,64,1024]{2,1,0:T(8,128)}, s32[4,2,32]{2,1,0:T(2,128)}, f32[256,256]{1,0:T(8,128)}) custom-call(f32[64,1024]{1,0:T(8,128)} %pts.3, f32[256,1024]{1,0:T(8,128)} %wts.1, f32[2,512,256]{2,1,0:T(8,128)} %interp.3, f32[14,512,256]{2,1,0:T(8,128)} %transfer.1, s32[1,256]{1,0:T(1,128)} %skg.1, ...), custom_call_target="tpu_custom_call" | custom-call | tf_op jit(solution)/shard_map/spread/pallas_call | solution.py:365
  56.2 0.0 copy-start
  56.2 0.0 copy-start.1
  56.2 1.1 convert_reduce_fusion
  57.4 0.1 copy.11
  57.4 0.1 select_n.70.times
  57.5 0.1 dynamic-slice_select_fusion
  57.6 0.1 copy.10
  57.7 0.1 copy.12
  57.8 0.1 log2.18.logs
  57.9 0.1 reshape.84.logs
  57.9 0.0 copy-start.2
  57.9 1.2 %copy-done.2 = f32[4,64,1024]{2,1,0:T(8,128)S(1)} copy-done((f32[4,64,1024]{2,1,0:T(8,128)S(1)}, f32[4,64,1024]{2,1,0:T(8,128)}, u32[]{:S(2)}) %copy-start.2) | copy-done | bytes 1048600
  59.2 0.0 copy-start.3
  59.2 18.8 %near.1.part = f32[8,256,512]{2,1,0:T(8,128)S(1)} custom-call(s32[96]{0:T(128)S(1)} %select_n.70.times, f32[96]{0:T(128)S(1)} %log2.18.logs, f32[3,2,5,64,1024]{4,3,2,1,0:T(8,128)} %get-tuple-element.10.cloud, f32[4,64,1024]{2,1,0:T(8,128)S(1)} %copy-done.2), custom_call_target="tpu_custom_call" | custom-call | tf_op jit(solution)/shard_map/near/pallas_call | solution.py:503
  78.0 0.0 copy-done
  78.0 0.0 copy-done.1
  78.0 0.0 copy-done.3
  78.0 37.7 %fold.1 = f32[256,1024]{1,0:T(8,128)S(1)} custom-call(f32[24]{0:T(128)S(1)} %reshape.84.logs, f32[8,256,512]{2,1,0:T(8,128)S(1)} %near.1.part, f32[256,256]{1,0:T(8,128)S(1)} %copy-done.3, f32[2,512,256]{2,1,0:T(8,128)S(1)} %copy-done, f32[3,2,5,64,1024]{4,3,2,1,0:T(8,128)} %get-tuple-element.10.cloud, f32[64,1024]{1,0:T(8,128)S(1)} %copy-done.1), custom_call_target="tpu_custom_call" | custom-call | tf_op jit(solution)/shard_map/fold/pallas_call | solution.py:655
  115.7 1.0 copy.14
  (4 shorter events, 0.0 us)
Async XLA Ops:
  56.2 21.8 %copy-start = (f32[2,512,256]{2,1,0:T(8,128)S(1)}, f32[2,512,256]{2,1,0:T(8,128)}, u32[]{:S(2)}) copy-start(f32[2,512,256]{2,1,0:T(8,128)} %interp.3) | copy-start | bytes 3145732
  56.2 21.8 %copy-start.1 = (f32[64,1024]{1,0:T(8,128)S(1)}, f32[64,1024]{1,0:T(8,128)}, u32[]{:S(2)}) copy-start(f32[64,1024]{1,0:T(8,128)} %pts.3) | copy-start | bytes 786436
  57.9 1.2 %copy-start.2 = (f32[4,64,1024]{2,1,0:T(8,128)S(1)}, f32[4,64,1024]{2,1,0:T(8,128)}, u32[]{:S(2)}) copy-start(f32[4,64,1024]{2,1,0:T(8,128)} %get-tuple-element.11.tgt) | copy-start | bytes 3145732
  59.2 18.9 %copy-start.3 = (f32[256,256]{1,0:T(8,128)S(1)}, f32[256,256]{1,0:T(8,128)}, u32[]{:S(2)}) copy-start(f32[256,256]{1,0:T(8,128)} %get-tuple-element.12.values) | copy-start | bytes 786436
